TPU v7x, 768 devices: a whole 4x8x12 slice. The times are simulated.
768 devices in a mesh: row: 96 (over z_lo, x, y), col: 8 (over z_hi, core).
Axes of the slice: x: 4, y: 8, z: 12 (z_hi: 4, z_lo: 3; z = z_hi * 3 + z_lo), core: 2. Of those that a mesh axis runs over, the one named last changes fastest.
Arguments:
- amplitudes: bfloat16 [49152, 4096], P('row', 'col'), may hold values from -6 to 6
- integrals: bfloat16 [1536, 4096], P('row', 'col'), may hold values from -0.09375 to 0.09375
- residual_in: float32 [49152, 1536], P('row', 'col'), may hold values from -6 to 6
- amp_live: int32 [384, 4], P('row'), may hold values 0 or 1
- int_live: int32 [4, 96], replicated, may hold values 0 or 1
Outputs:
- residual_out: float32 [49152, 1536], P('row', 'col')
All inputs are finite; a program needn't handle non-finite values. No bound on the sum of `amp_live` on one device may be relied on, other than what follows from the above.
Results may differ from a plain program's by a relative error of at most 0.0003.
Values may be sent and summed in bfloat16 or wider, within the bound.
No kernel may reach another device: no remote copies, remote signals or barrier semaphores. Data moves between devices by JAX's collectives and lax.ppermute only.
A program may use at most 32 MiB of HBM per device.

v0:
```python
import jax
import jax.numpy as jnp
from jax import lax
from jax.sharding import PartitionSpec as P

KTILE = 1024


def masked_shards(amplitudes, integrals, amp_live, int_live):
    local_k = amplitudes.shape[1]
    ktiles = amp_live.shape[1]
    first = lax.axis_index("col") * local_k
    ktile_of = (first + jnp.arange(local_k, dtype=jnp.int32)) // KTILE
    onehot_k = (ktile_of[:, None] == jnp.arange(ktiles, dtype=jnp.int32)[None, :]).astype(
        jnp.float32
    )
    amp_rows = jnp.dot(amp_live.astype(jnp.float32), jnp.transpose(onehot_k))
    row_tile = amplitudes.shape[0] // amp_live.shape[0]
    amp_mask = jnp.repeat(amp_rows, row_tile, axis=0).astype(jnp.bfloat16)
    live_amp = amplitudes * amp_mask
    row_pick = (jnp.arange(int_live.shape[1], dtype=jnp.int32) == lax.axis_index("row")).astype(
        jnp.float32
    )
    k_keep = jnp.dot(int_live.astype(jnp.float32), row_pick)
    int_keep = jnp.dot(onehot_k, k_keep).astype(jnp.bfloat16)
    live_int = integrals * int_keep[None, :]
    return (live_amp, live_int)


def contract(left, right):
    return lax.dot_general(
        left, right, (((1,), (1,)), ((), ())), preferred_element_type=jnp.float32
    )


def shards(amplitudes, integrals, residual_in, amp_live, int_live):
    live_amp, live_int = masked_shards(amplitudes, integrals, amp_live, int_live)
    all_int = lax.all_gather(live_int, "row", axis=0, tiled=True)
    full_amp = lax.all_gather(live_amp, "col", axis=1, tiled=True)
    own_int = lax.all_to_all(all_int, "col", split_axis=0, concat_axis=1, tiled=True)
    ladder = contract(full_amp, own_int)
    return residual_in + ladder


def solution(mesh):
    in_specs = (P("row", "col"), P("row", "col"), P("row", "col"), P("row", None), P())
    out_specs = P("row", "col")
    return jax.shard_map(shards, mesh=mesh, in_specs=in_specs, out_specs=out_specs, check_vma=False)
```

profile of v0, /device:TPU:63, one launch (start us, length us, event | category | flops | bytes accessed | tf_op | source)
XLA Modules:
  0.0 674.7 jit_solution(2744806632468271390)
XLA Ops:
  6.5 0.0 all-gather.5.cloned.1.call-start
  6.5 0.9 fusion.1
  7.5 1.3 broadcast_multiply_fusion
  8.8 0.0 all-gather.5.cloned.1.call-update
  8.8 0.0 all-gather.3.cloned.1.call-start
  8.9 0.9 fusion
  9.8 1.9 bitcast_multiply_fusion
  11.7 0.0 all-gather.3.cloned.1.call-update
  11.7 380.7 %all-gather.5.cloned.1.call-done = bf16[1536,512]{1,0:T(8,128)(2,1)} async-done(((bf16[16,512]{1,0:T(8,128)(2,1)}), bf16[1536,512]{1,0:T(8,128)(2,1)}) %all-gather.5.cloned.1.call-update) | async-done | bytes 1572880 | tf_op jit(solution)/shard_map/all_gather | solution.py:38
  392.4 151.0 %all_to_all.19 = bf16[8,192,512]{2,1,0:T(8,128)(2,1)S(1)} all-to-all(bf16[8,192,512]{2,1,0:T(8,128)(2,1)} %bitcast.21), channel_id=1, replica_groups=mesh['row'=96,'col'=8] {'col'}, dimensions={0} | all-to-all | bytes 3145728 | tf_op jit(solution)/shard_map/all_to_all | solution.py:40
  543.4 0.0 copy-start
  543.4 0.2 copy.8
  543.6 119.9 %all-gather.3.cloned.1.call-done = bf16[512,4096]{1,0:T(8,128)(2,1)} async-done(((bf16[512,512]{1,0:T(8,128)(2,1)}), bf16[512,4096]{1,0:T(8,128)(2,1)}) %all-gather.3.cloned.1.call-update) | async-done | bytes 4194320 | tf_op jit(solution)/shard_map/all_gather | solution.py:39
  663.4 0.0 copy-done
  663.4 4.5 convolution_add_fusion
  (2 shorter events, 0.0 us)
Async XLA Ops:
  6.5 385.9 %all-gather.5.cloned.1.call-start = ((), (), s32[]{:S(2)}) async-start(), calls=%async_computation.2 | async-start | bytes 1589248 | tf_op jit(solution)/shard_map/all_gather | solution.py:38
  8.8 654.6 %all-gather.3.cloned.1.call-start = ((), (), s32[]{:S(2)}) async-start(), calls=%async_computation.1 | async-start | bytes 4718592 | tf_op jit(solution)/shard_map/all_gather | solution.py:39
  543.4 120.0 %copy-start = (f32[512,192]{0,1:T(8,128)S(1)}, f32[512,192]{0,1:T(8,128)}, u32[]{:S(2)}) copy-start(f32[512,192]{0,1:T(8,128)} %param.7) | copy-start | bytes 1179652
Sparse Core Ops, SparseCore 0:
  9.7 382.6 all-gather.4
  394.8 268.5 all-gather.2
where the time goes:
time: 675 us
  waiting for transfers between devices  501 us (74%)
  blocking collectives  151 us (22%)
  between operations  13.4 us (2%)
    all_gather x1, waiting for transfers between devices, shards(): all_int = lax.all_gather(live_int, 'row', axis=0, tiled=True)  381 us
    all_to_all x1, blocking collectives, shards(): lax.all_to_all(all_int, 'col', split_axis=0, concat_axis=1, tiled=True)  151 us
    all_gather x1, waiting for transfers between devices, shards(): full_amp = lax.all_gather(live_amp, 'col', axis=1, tiled=True)  120 us
  transfers between devices with their start and end apart: 2, of which 2 were waited for; matrix products, arithmetic and copies ran while one was open for 0% of the time, Pallas kernels for 0%

commit v1 on v0

v1 whole, which is shorter than its diff:
```python
import numpy as np
import jax
import jax.numpy as jnp
from jax import lax
from jax.sharding import Mesh, PartitionSpec as P

AXES = ("zl", "x", "yh", "yl", "zh", "core")
SIZES = (3, 4, 4, 2, 4, 2)
ROW = ("zl", "x", "yh", "yl")
COL = ("zh", "core")
SCALE = 64.0


def blocks(q):
    return ((q, q), ((q + 1) % 4, q), ((q - 1) % 4, q), (q, (q + 2) % 4))


def deal():
    pairs = []
    for zl, x, yh, yl, q, j in np.ndindex(*SIZES):
        kt, n = blocks(q)[x]
        rp = 12 * (2 * n + j) + zl * 4 + yh
        source = rp * 8 + kt * 2 + yl
        target = int(np.ravel_multi_index((zl, x, yh, yl, q, j), SIZES))
        pairs.append((source, target))
    return pairs


def contract(left, right):
    return lax.dot_general(
        left, right, (((1,), (1,)), ((), ())), preferred_element_type=jnp.float32
    )


def shift(value, by):
    return lax.ppermute(value, "zh", [(i, (i + by) % 4) for i in range(4)])


def swap(value):
    return lax.ppermute(value, "core", [(0, 1), (1, 0)])


def gather(piece, axes, peers):
    copies = jnp.broadcast_to(piece[None], (peers,) + piece.shape)
    return lax.all_to_all(copies, axes, split_axis=0, concat_axis=0, tiled=True)


def shards(amplitudes, integrals, residual_in, amp_live, int_live):
    q, j = lax.axis_index("zh"), lax.axis_index("core")
    piece = lax.ppermute(integrals, AXES, deal())
    mine = amplitudes
    up, down = shift(amplitudes, -1), shift(amplitudes, 1)
    other = swap(mine)
    some = gather(piece, ("zl", "yh"), 12).reshape(192, 512)
    every = gather(some, ("x", "yl"), 8)
    up_other, down_other = swap(up), swap(down)

    def product(slot, own, sibling, kt, n):
        first = jnp.where(j == 0, every[2 * slot], every[2 * slot + 1])
        second = jnp.where(j == 0, every[2 * slot + 1], every[2 * slot])
        total = contract(first, own) + contract(second, sibling)
        rows = lax.dynamic_slice(int_live, (kt, 12 * (2 * n + j)), (1, 12))
        cols = lax.dynamic_slice(amp_live, (0, kt), (4, 1))
        keep_rows = jnp.repeat(rows.reshape(12), 16).astype(jnp.float32)
        keep_cols = jnp.repeat(cols.reshape(4), 128).astype(jnp.float32)
        return total * (keep_rows[:, None] * keep_cols[None, :])

    far = product(3, mine, other, q, (q + 2) % 4)
    arrived = shift((far * SCALE).astype(jnp.float16), 2)
    near = product(0, mine, other, q, q)
    near = near + product(1, up, up_other, (q + 1) % 4, q)
    near = near + product(2, down, down_other, (q + 3) % 4, q)
    total = near + arrived.astype(jnp.float32) * (1.0 / SCALE)
    return residual_in + jnp.transpose(total)


def solution(mesh):
    fine = Mesh(mesh.devices.reshape(SIZES), AXES)
    in_specs = (P(ROW, COL), P(ROW, COL), P(ROW, COL), P(ROW, None), P())
    return jax.shard_map(
        shards, mesh=fine, in_specs=in_specs, out_specs=P(ROW, COL), check_vma=False
    )
```

time: 675 us -> 123 us (0.18)
  the two profiles are of different devices: /device:TPU:63 before, /device:TPU:67 now
where the time goes in v1:
time: 123 us; the launch traced here: 122 us
  waiting for transfers between devices  49 us (40%)
  starting transfers between devices  42.1 us (34%)
  blocking collectives  20.9 us (17%)
  matrix products  7.64 us (6%)
  local copies, waits for them, and re-layouts  2.05 us (2%)
    ppermute x3, waiting for transfers between devices, shift(): return lax.ppermute(value, 'zh', [(i, (i + by) % 4) for i in range(4)])  47.9 us
    all_to_all x1, blocking collectives, gather(): return lax.all_to_all(copies, axes, split_axis=0, concat_axis=0, tiled=True)  20.9 us
    ppermute x3, starting transfers between devices, shift(): return lax.ppermute(value, 'zh', [(i, (i + by) % 4) for i in range(4)])  17.1 us
    ppermute x1, starting transfers between devices, shards(): piece = lax.ppermute(integrals, AXES, deal())  10.8 us
    ppermute x3, starting transfers between devices, swap(): return lax.ppermute(value, 'core', [(0, 1), (1, 0)])  9.14 us
    dot_general x8, matrix products, contract(): lax.dot_general(left, right, (((1,), (1,)), ((), ())), preferred_element_...  7.64 us
    all_to_all x1, starting transfers between devices, gather(): return lax.all_to_all(copies, axes, split_axis=0, concat_axis=0, tiled=True)  5.16 us
  transfers between devices with their start and end apart: 8, of which 4 were waited for; matrix products, arithmetic and copies ran while one was open for 6% of the time, Pallas kernels for 0%

profile of v1, /device:TPU:67, one launch (start us, length us, event | category | flops | bytes accessed | tf_op | source)
XLA Modules:
  0.0 122.3 jit_solution(8537858736872388821)
XLA Ops:
  0.0 10.8 %collective-permute-start = (bf16[16,512]{1,0:T(8,128)(2,1)}, bf16[16,512]{1,0:T(8,128)(2,1)S(1)}, u32[]{:S(2)}, u32[]{:S(2)}) collective-permute-start(bf16[16,512]{1,0:T(8,128)(2,1)} %param.6), channel_id=1, source_target_pairs={{0,0},{96,1},{194,2},{290,3},{388,4},{484,5},{582,6},{678,7},{1,8}... | collective-permute-start | bytes 49160 | tf_op jit(solution)/shard_map/ppermute | solution.py:50
  10.8 1.1 collective-permute-done
  11.8 20.9 %all_to_all.10 = bf16[12,16,512]{2,1,0:T(8,128)(2,1)S(1)} all-to-all(bf16[12,16,512]{2,1,0:T(8,128)(2,1)S(1)} %broadcast_in_dim.20), channel_id=1, replica_groups=mesh['zl'=3,'x'=4,'yh'=4,'yl'=2,'zh'=4,'core'=2] {'zl','yh'}, dimensions={0} | all-to-all | bytes 393216 | tf_op jit(solution)/shard_map/all_to_all | solution.py:45
  32.8 1.3 %broadcast_in_dim.22 = bf16[8,192,512]{2,1,0:T(8,128)(2,1)} broadcast(bf16[192,512]{1,0:T(8,128)(2,1)S(1)} %bitcast.51), dimensions={1,2} | broadcast | bytes 1769472 | tf_op jit(solution)/shard_map/broadcast_in_dim | solution.py:44
  34.1 5.2 %all-to-all-start.1 = ((bf16[8,192,512]{2,1,0:T(8,128)(2,1)}), bf16[8,192,512]{2,1,0:T(8,128)(2,1)S(1)}, u32[]{:S(2)}, u32[]{:S(2)}) async-start(bf16[8,192,512]{2,1,0:T(8,128)(2,1)} %broadcast_in_dim.22), calls=%async_computation.1 | async-start | bytes 3145728 | tf_op jit(solution)/shard_map/all_to_all | solution.py:45
  39.2 4.5 %collective-permute-start.1 = (bf16[512,512]{1,0:T(8,128)(2,1)S(1)}, bf16[512,512]{1,0:T(8,128)(2,1)}, u32[]{:S(2)}, u32[]{:S(2)}) collective-permute-start(bf16[512,512]{1,0:T(8,128)(2,1)S(1)} %copy-done), channel_id=1, source_target_pairs={{0,1},{1,0},{2,3},{3,2},{4,5},{5,4},{6,7},{7,6},{8,9},{9,8},{10,11... | collective-permute-start | bytes 1572872 | tf_op jit(solution)/shard_map/ppermute | solution.py:40
  43.7 10.5 %collective-permute-start.4 = (bf16[512,512]{1,0:T(8,128)(2,1)S(1)}, bf16[512,512]{1,0:T(8,128)(2,1)}, u32[]{:S(2)}, u32[]{:S(2)}) collective-permute-start(bf16[512,512]{1,0:T(8,128)(2,1)S(1)} %copy-done), channel_id=1, source_target_pairs={{0,2},{2,4},{4,6},{6,0},{1,3},{3,5},{5,7},{7,1},{8,10},{10,12},{12... | collective-permute-start | bytes 1572872 | tf_op jit(solution)/shard_map/ppermute | solution.py:36
  54.2 1.9 %collective-permute-start.2 = (bf16[512,512]{1,0:T(8,128)(2,1)S(1)}, bf16[512,512]{1,0:T(8,128)(2,1)S(1)}, u32[]{:S(2)}, u32[]{:S(2)}) collective-permute-start(bf16[512,512]{1,0:T(8,128)(2,1)S(1)} %copy-done), channel_id=1, source_target_pairs={{0,6},{2,0},{4,2},{6,4},{1,7},{3,1},{5,3},{7,5},{8,14},{10,8},{12,... | collective-permute-start | bytes 1572872 | tf_op jit(solution)/shard_map/ppermute | solution.py:36
  56.2 0.2 convert_reduce_fusion.1
  56.5 0.1 convert_bitcast_fusion.2
  57.3 31.4 %collective-permute-done.4 = bf16[512,512]{1,0:T(8,128)(2,1)} collective-permute-done((bf16[512,512]{1,0:T(8,128)(2,1)S(1)}, bf16[512,512]{1,0:T(8,128)(2,1)}, u32[]{:S(2)}, u32[]{:S(2)}) %collective-permute-start.4) | collective-permute-done | bytes 524320 | tf_op jit(solution)/shard_map/ppermute | solution.py:36
  88.7 2.3 %collective-permute-start.5 = (bf16[512,512]{1,0:T(8,128)(2,1)}, bf16[512,512]{1,0:T(8,128)(2,1)}, u32[]{:S(2)}, u32[]{:S(2)}) collective-permute-start(bf16[512,512]{1,0:T(8,128)(2,1)} %collective-permute-done.4), channel_id=1, source_target_pairs={{0,1},{1,0},{2,3},{3,2},{4,5},{5,4},{6,7},{7,6},{8,9},{9,8},{10,11... | collective-permute-start | bytes 1572872 | tf_op jit(solution)/shard_map/ppermute | solution.py:40
  91.0 4.2 %collective-permute-done.2 = bf16[512,512]{1,0:T(8,128)(2,1)S(1)} collective-permute-done((bf16[512,512]{1,0:T(8,128)(2,1)S(1)}, bf16[512,512]{1,0:T(8,128)(2,1)S(1)}, u32[]{:S(2)}, u32[]{:S(2)}) %collective-permute-start.2) | collective-permute-done | bytes 524320 | tf_op jit(solution)/shard_map/ppermute | solution.py:36
  95.2 2.4 %collective-permute-start.3 = (bf16[512,512]{1,0:T(8,128)(2,1)S(1)}, bf16[512,512]{1,0:T(8,128)(2,1)S(1)}, u32[]{:S(2)}, u32[]{:S(2)}) collective-permute-start(bf16[512,512]{1,0:T(8,128)(2,1)S(1)} %collective-permute-done.2), channel_id=1, source_target_pairs={{0,1},{1,0},{2,3},{3,2},{4,5},{5,4},{6,7},{7,6},{8,9},{9,8},{10,11... | collective-permute-start | bytes 1572872 | tf_op jit(solution)/shard_map/ppermute | solution.py:40
  97.6 0.3 fusion.12
  97.9 1.4 %fusion.10 = f16[192,512]{1,0:T(8,128)(2,1)S(1)} fusion(f32[192,512]{1,0:T(8,128)S(1)} %fusion.12, bf16[512,512]{1,0:T(8,128)(2,1)} %collective-permute-done.1, f32[192]{0:T(256)S(1)} %convert_element_type.125, f32[512]{0:T(512)S(1)} %broadcast_bitcast_fusion.2, pred[]{:T(512)S(6)} %eq.6, bf16[8,192,512]{2,1,0:T(8,128)(2,1)S(1)} %all-to-all-done.1), kind=kOutput, calls=%fused_computation.14 | convolution fusion | flops 101253120 | bytes 1510401 | tf_op jit(solution)/shard_map/dot_general | solution.py:30
  99.3 4.6 %collective-permute-start.6 = (f16[192,512]{1,0:T(8,128)(2,1)S(1)}, f16[192,512]{1,0:T(8,128)(2,1)S(1)}, u32[]{:S(2)}, u32[]{:S(2)}) collective-permute-start(f16[192,512]{1,0:T(8,128)(2,1)S(1)} %fusion.10), channel_id=1, source_target_pairs={{0,4},{2,6},{4,0},{6,2},{1,5},{3,7},{5,1},{7,3},{8,12},{10,14},{12... | collective-permute-start | bytes 589832 | tf_op jit(solution)/shard_map/ppermute | solution.py:36
  103.9 0.3 fusion.21
  104.3 1.4 %fusion = f32[192,512]{1,0:T(8,128)S(1)} fusion(f32[192,512]{1,0:T(8,128)S(1)} %fusion.21, bf16[512,512]{1,0:T(8,128)(2,1)} %collective-permute-done.1, f32[512]{0:T(512)S(1)} %broadcast_bitcast_fusion.2, f32[192]{0:T(256)S(1)} %convert_element_type.107, pred[]{:T(512)S(6)} %eq.6, bf16[8,192,512]{2,1,0:T(8,128)(2,1)S(1)} %all-to-all-done.1), kind=kOutput, calls=%fused_computation.4 | convolution fusion | flops 101056512 | bytes 1707009 | tf_op jit(solution)/shard_map/dot_general | solution.py:30
  105.6 1.4 %fusion.15 = f32[192,512]{1,0:T(8,128)S(1)} fusion(bf16[512,512]{1,0:T(8,128)(2,1)} %collective-permute-done.4, pred[]{:T(512)S(6)} %eq.6, bf16[8,192,512]{2,1,0:T(8,128)(2,1)S(1)} %all-to-all-done.1), kind=kOutput, calls=%fused_computation.19 | convolution fusion | flops 100761600 | bytes 1310721 | tf_op jit(solution)/shard_map/dot_general | solution.py:30
  107.0 1.4 %fusion.7 = f32[192,512]{1,0:T(8,128)S(1)} fusion(f32[192,512]{1,0:T(8,128)S(1)} %fusion.15, bf16[512,512]{1,0:T(8,128)(2,1)} %collective-permute-done.5, f32[512]{0:T(512)S(1)} %get-tuple-element.12, f32[192]{0:T(256)S(1)} %convert_element_type.119, pred[]{:T(512)S(6)} %eq.6, bf16[8,192,512]{2,1,0:T(8,128)(2,1)S(1)} %all-to-all-done.1), kind=kOutput, calls=%fused_computation.11 | convolution fusion | flops 101056512 | bytes 1707009 | tf_op jit(solution)/shard_map/dot_general | solution.py:30
  108.5 0.3 fusion.18
  108.8 12.3 %collective-permute-done.6 = f16[192,512]{1,0:T(8,128)(2,1)S(1)} collective-permute-done((f16[192,512]{1,0:T(8,128)(2,1)S(1)}, f16[192,512]{1,0:T(8,128)(2,1)S(1)}, u32[]{:S(2)}, u32[]{:S(2)}) %collective-permute-start.6) | collective-permute-done | bytes 196640 | tf_op jit(solution)/shard_map/ppermute | solution.py:36
  121.1 1.1 fusion.6
  (23 shorter events, 0.8 us)
Async XLA Ops:
  0.0 11.8 %collective-permute-start = (bf16[16,512]{1,0:T(8,128)(2,1)}, bf16[16,512]{1,0:T(8,128)(2,1)S(1)}, u32[]{:S(2)}, u32[]{:S(2)}) collective-permute-start(bf16[16,512]{1,0:T(8,128)(2,1)} %param.6), channel_id=1, source_target_pairs={{0,0},{96,1},{194,2},{290,3},{388,4},{484,5},{582,6},{678,7},{1,8}... | collective-permute-start | bytes 49160 | tf_op jit(solution)/shard_map/ppermute | solution.py:50
  34.1 5.2 %copy-start = (bf16[512,512]{1,0:T(8,128)(2,1)S(1)}, bf16[512,512]{1,0:T(8,128)(2,1)}, u32[]{:S(2)}) copy-start(bf16[512,512]{1,0:T(8,128)(2,1)} %param.5) | copy-start | bytes 1572868
  34.1 22.2 %copy-start.2 = (s32[4,4]{1,0:T(4,128)S(1)}, s32[4,4]{1,0:T(4,128)}, u32[]{:S(2)}) copy-start(s32[4,4]{1,0:T(4,128)} %param.8) | copy-start | bytes 196
  34.1 22.5 %copy-start.3 = (s32[4,96]{1,0:T(4,128)S(1)}, s32[4,96]{1,0:T(4,128)}, u32[]{:S(2)}) copy-start(s32[4,96]{1,0:T(4,128)} %param.9) | copy-start | bytes 4612
  34.1 63.5 %all-to-all-start.1 = ((bf16[8,192,512]{2,1,0:T(8,128)(2,1)}), bf16[8,192,512]{2,1,0:T(8,128)(2,1)S(1)}, u32[]{:S(2)}, u32[]{:S(2)}) async-start(bf16[8,192,512]{2,1,0:T(8,128)(2,1)} %broadcast_in_dim.22), calls=%async_computation.1 | async-start | bytes 3145728 | tf_op jit(solution)/shard_map/all_to_all | solution.py:45
  39.2 58.7 %collective-permute-start.1 = (bf16[512,512]{1,0:T(8,128)(2,1)S(1)}, bf16[512,512]{1,0:T(8,128)(2,1)}, u32[]{:S(2)}, u32[]{:S(2)}) collective-permute-start(bf16[512,512]{1,0:T(8,128)(2,1)S(1)} %copy-done), channel_id=1, source_target_pairs={{0,1},{1,0},{2,3},{3,2},{4,5},{5,4},{6,7},{7,6},{8,9},{9,8},{10,11... | collective-permute-start | bytes 1572872 | tf_op jit(solution)/shard_map/ppermute | solution.py:40
  43.7 45.0 %collective-permute-start.4 = (bf16[512,512]{1,0:T(8,128)(2,1)S(1)}, bf16[512,512]{1,0:T(8,128)(2,1)}, u32[]{:S(2)}, u32[]{:S(2)}) collective-permute-start(bf16[512,512]{1,0:T(8,128)(2,1)S(1)} %copy-done), channel_id=1, source_target_pairs={{0,2},{2,4},{4,6},{6,0},{1,3},{3,5},{5,7},{7,1},{8,10},{10,12},{12... | collective-permute-start | bytes 1572872 | tf_op jit(solution)/shard_map/ppermute | solution.py:36
  54.2 41.0 %collective-permute-start.2 = (bf16[512,512]{1,0:T(8,128)(2,1)S(1)}, bf16[512,512]{1,0:T(8,128)(2,1)S(1)}, u32[]{:S(2)}, u32[]{:S(2)}) collective-permute-start(bf16[512,512]{1,0:T(8,128)(2,1)S(1)} %copy-done), channel_id=1, source_target_pairs={{0,6},{2,0},{4,2},{6,4},{1,7},{3,1},{5,3},{7,5},{8,14},{10,8},{12,... | collective-permute-start | bytes 1572872 | tf_op jit(solution)/shard_map/ppermute | solution.py:36
  88.7 18.3 %collective-permute-start.5 = (bf16[512,512]{1,0:T(8,128)(2,1)}, bf16[512,512]{1,0:T(8,128)(2,1)}, u32[]{:S(2)}, u32[]{:S(2)}) collective-permute-start(bf16[512,512]{1,0:T(8,128)(2,1)} %collective-permute-done.4), channel_id=1, source_target_pairs={{0,1},{1,0},{2,3},{3,2},{4,5},{5,4},{6,7},{7,6},{8,9},{9,8},{10,11... | collective-permute-start | bytes 1572872 | tf_op jit(solution)/shard_map/ppermute | solution.py:40
  95.2 13.6 %collective-permute-start.3 = (bf16[512,512]{1,0:T(8,128)(2,1)S(1)}, bf16[512,512]{1,0:T(8,128)(2,1)S(1)}, u32[]{:S(2)}, u32[]{:S(2)}) collective-permute-start(bf16[512,512]{1,0:T(8,128)(2,1)S(1)} %collective-permute-done.2), channel_id=1, source_target_pairs={{0,1},{1,0},{2,3},{3,2},{4,5},{5,4},{6,7},{7,6},{8,9},{9,8},{10,11... | collective-permute-start | bytes 1572872 | tf_op jit(solution)/shard_map/ppermute | solution.py:40
  99.3 21.8 %collective-permute-start.6 = (f16[192,512]{1,0:T(8,128)(2,1)S(1)}, f16[192,512]{1,0:T(8,128)(2,1)S(1)}, u32[]{:S(2)}, u32[]{:S(2)}) collective-permute-start(f16[192,512]{1,0:T(8,128)(2,1)S(1)} %fusion.10), channel_id=1, source_target_pairs={{0,4},{2,6},{4,0},{6,2},{1,5},{3,7},{5,1},{7,3},{8,12},{10,14},{12... | collective-permute-start | bytes 589832 | tf_op jit(solution)/shard_map/ppermute | solution.py:36
  107.0 14.1 %copy-start.1 = (f32[512,192]{0,1:T(8,128)S(1)}, f32[512,192]{0,1:T(8,128)}, u32[]{:S(2)}) copy-start(f32[512,192]{0,1:T(8,128)} %param.7) | copy-start | bytes 1179652

commit v2 on v1

v2 whole, which is shorter than its diff:
```python
import numpy as np
import jax
import jax.numpy as jnp
from jax import lax
from jax.sharding import Mesh, PartitionSpec as P

AXES = ("zl", "x", "yh", "yl", "zh", "core")
SIZES = (3, 4, 4, 2, 4, 2)
ROW = ("zl", "x", "yh", "yl")
COL = ("zh", "core")
SCALE = 64.0
CHUNKS = 1


def deal():
    pairs = []
    for zl, x, yh, yl, q, j in np.ndindex(*SIZES):
        source_row = 12 * (2 * x + j) + zl * 4 + yh
        source = source_row * 8 + q * 2 + (j ^ yl)
        target = int(np.ravel_multi_index((zl, x, yh, yl, q, j), SIZES))
        pairs.append((source, target))
    return pairs


def contract(left, right):
    return lax.dot_general(
        left, right, (((1,), (1,)), ((), ())), preferred_element_type=jnp.float32
    )


def swap(value):
    return lax.ppermute(value, "core", [(0, 1), (1, 0)])


def gather(piece, axes, peers):
    copies = jnp.broadcast_to(piece[None], (peers,) + piece.shape)
    return lax.all_to_all(copies, axes, split_axis=0, concat_axis=0, tiled=True)


def shards(amplitudes, integrals, residual_in, amp_live, int_live):
    q, j = lax.axis_index("zh"), lax.axis_index("core")
    piece = lax.ppermute(integrals, AXES, deal())
    other = swap(amplitudes)
    some = gather(piece, ("zl", "yh"), 12).reshape(192, 512)
    keep_int = lax.dynamic_slice(int_live, (q, 0), (1, 96)).reshape(4, 2, 12)
    keep_int = lax.dynamic_slice(keep_int, (0, j, 0), (4, 1, 12)).reshape(4, 12)
    keep_int = jnp.repeat(keep_int, 16, axis=1).astype(jnp.float32)
    keep_amp = lax.dynamic_slice(amp_live, (0, q), (4, 1)).reshape(4)
    keep_amp = jnp.repeat(keep_amp, 128).astype(jnp.float32)
    size = 192 // CHUNKS
    outs = []
    for part in range(CHUNKS):
        rows = slice(part * size, (part + 1) * size)
        every = gather(some[rows], ("yl", "x"), 8).reshape(2, 4 * size, 512)
        total = contract(every[0], amplitudes) + contract(every[1], other)
        total = total.reshape(4, size, 512)
        total = total * (keep_int[:, rows, None] * keep_amp[None, None, :])
        sent = (total * SCALE).astype(jnp.float16)
        came = lax.all_to_all(sent, "zh", split_axis=0, concat_axis=0, tiled=True)
        own = lax.dynamic_slice(total, (q, 0, 0), (1, size, 512))[0]
        for kt in range(4):
            term = came[kt].astype(jnp.float32) * (1.0 / SCALE)
            own = own + jnp.where(kt == q, 0.0, term)
        outs.append(own)
    total = jnp.concatenate(outs, axis=0)
    return residual_in + jnp.transpose(total)


def solution(mesh):
    fine = Mesh(mesh.devices.reshape(SIZES), AXES)
    in_specs = (P(ROW, COL), P(ROW, COL), P(ROW, COL), P(ROW, None), P())
    return jax.shard_map(
        shards, mesh=fine, in_specs=in_specs, out_specs=P(ROW, COL), check_vma=False
    )
```

time: 123 us -> 109 us (0.89)
  the two profiles are of different devices: /device:TPU:67 before, /device:TPU:10 now
where the time goes in v2:
time: 109 us; the launch traced here: 108 us
  waiting for transfers between devices  49.9 us (46%)
  starting transfers between devices  31.6 us (29%)
  blocking collectives  21.3 us (20%)
  other arithmetic  2.36 us (2%)
  local copies, waits for them, and re-layouts  1.83 us (2%)
  matrix products  1.22 us (1%)
    all_to_all x1, waiting for transfers between devices, shards(): came = lax.all_to_all(sent, 'zh', split_axis=0, concat_axis=0, tiled=True)  33.2 us
    all_to_all x1, blocking collectives, gather(): return lax.all_to_all(copies, axes, split_axis=0, concat_axis=0, tiled=True)  21.3 us
    all_to_all x1, starting transfers between devices, shards(): came = lax.all_to_all(sent, 'zh', split_axis=0, concat_axis=0, tiled=True)  16.6 us
    all_to_all x1, waiting for transfers between devices, gather(): return lax.all_to_all(copies, axes, split_axis=0, concat_axis=0, tiled=True)  15.1 us
    ppermute x1, starting transfers between devices, shards(): piece = lax.ppermute(integrals, AXES, deal())  7.19 us
    all_to_all x1, starting transfers between devices, gather(): return lax.all_to_all(copies, axes, split_axis=0, concat_axis=0, tiled=True)  5.88 us
  transfers between devices with their start and end apart: 4, of which 3 were waited for; matrix products, arithmetic and copies ran while one was open for 1% of the time, Pallas kernels for 0%

profile of v2, /device:TPU:10, one launch (start us, length us, event | category | flops | bytes accessed | tf_op | source)
XLA Modules:
  0.0 108.4 jit_solution(6729196890936366896)
XLA Ops:
  0.0 0.0 copy-start
  0.0 7.2 %collective-permute-start = (bf16[16,512]{1,0:T(8,128)(2,1)}, bf16[16,512]{1,0:T(8,128)(2,1)S(1)}, u32[]{:S(2)}, u32[]{:S(2)}) collective-permute-start(bf16[16,512]{1,0:T(8,128)(2,1)} %param.6), channel_id=1, source_target_pairs={{0,0},{97,1},{2,2},{99,3},{4,4},{101,5},{6,6},{103,7},{1,8},{96,9}... | collective-permute-start | bytes 49160 | tf_op jit(solution)/shard_map/ppermute | solution.py:42
  7.2 1.6 %collective-permute-done = bf16[16,512]{1,0:T(8,128)(2,1)S(1)} collective-permute-done((bf16[16,512]{1,0:T(8,128)(2,1)}, bf16[16,512]{1,0:T(8,128)(2,1)S(1)}, u32[]{:S(2)}, u32[]{:S(2)}) %collective-permute-start) | collective-permute-done | bytes 16416 | tf_op jit(solution)/shard_map/ppermute | solution.py:42
  8.9 21.3 %all_to_all.15 = bf16[12,16,512]{2,1,0:T(8,128)(2,1)S(1)} all-to-all(bf16[12,16,512]{2,1,0:T(8,128)(2,1)S(1)} %broadcast_in_dim.28), channel_id=1, replica_groups=mesh['zl'=3,'x'=4,'yh'=4,'yl'=2,'zh'=4,'core'=2] {'zl','yh'}, dimensions={0} | all-to-all | bytes 393216 | tf_op jit(solution)/shard_map/all_to_all | solution.py:37
  30.2 1.3 %broadcast_in_dim.30 = bf16[8,192,512]{2,1,0:T(8,128)(2,1)} broadcast(bf16[192,512]{1,0:T(8,128)(2,1)S(1)} %bitcast.18), dimensions={1,2} | broadcast | bytes 1769472 | tf_op jit(solution)/shard_map/broadcast_in_dim | solution.py:36
  31.5 5.9 %all-to-all-start.1 = ((bf16[8,192,512]{2,1,0:T(8,128)(2,1)}), bf16[8,192,512]{2,1,0:T(8,128)(2,1)S(1)}, u32[]{:S(2)}, u32[]{:S(2)}) async-start(bf16[8,192,512]{2,1,0:T(8,128)(2,1)} %broadcast_in_dim.30), calls=%async_computation.1 | async-start | bytes 3145728 | tf_op jit(solution)/shard_map/all_to_all | solution.py:37
  37.4 0.0 copy-done.1
  37.4 1.9 %collective-permute-start.1 = (bf16[512,512]{1,0:T(8,128)(2,1)S(1)}, bf16[512,512]{1,0:T(8,128)(2,1)S(1)}, u32[]{:S(2)}, u32[]{:S(2)}) collective-permute-start(bf16[512,512]{1,0:T(8,128)(2,1)S(1)} %copy-done.1), channel_id=1, source_target_pairs={{0,1},{1,0},{2,3},{3,2},{4,5},{5,4},{6,7},{7,6},{8,9},{9,8},{10,11... | collective-permute-start | bytes 1572872 | tf_op jit(solution)/shard_map/ppermute | solution.py:32
  39.3 0.0 copy-done
  39.3 0.1 reshape.57
  39.4 0.1 broadcast_in_dim.31
  39.5 0.1 convert_element_type.49
  39.6 0.0 copy-done.3
  39.6 0.2 convert_reduce_fusion
  39.8 0.1 broadcast_bitcast_fusion
  39.8 15.1 %all-to-all-done.1 = bf16[8,192,512]{2,1,0:T(8,128)(2,1)S(1)} async-done(((bf16[8,192,512]{2,1,0:T(8,128)(2,1)}), bf16[8,192,512]{2,1,0:T(8,128)(2,1)S(1)}, u32[]{:S(2)}, u32[]{:S(2)}) %all-to-all-start.1) | async-done | bytes 1572896 | tf_op jit(solution)/shard_map/all_to_all | solution.py:37
  54.9 0.2 fusion.1
  55.1 0.6 fusion.2
  55.7 0.0 collective-permute-done.1
  55.7 0.6 convolution_add_fusion
  56.4 1.2 %multiply_convert_fusion = (f16[4,192,512]{2,1,0:T(8,128)(2,1)}, f32[4,192,512]{2,1,0:T(8,128)S(1)}) fusion(f32[4,192,512]{2,1,0:T(8,128)S(1)} %bitcast.15, f32[512]{0:T(512)S(1)} %broadcast_bitcast_fusion, f32[4,192]{1,0:T(4,128)S(1)} %convert_element_type.49), kind=kLoop, calls=%fused_computation | loop fusion | flops 1572864 | bytes 3937280 | tf_op jit(solution)/shard_map/convert_element_type | solution.py:58
  57.6 16.6 %all-to-all-start.2 = ((f16[4,192,512]{2,1,0:T(8,128)(2,1)}), f16[4,192,512]{2,1,0:T(8,128)(2,1)S(1)}, u32[]{:S(2)}, u32[]{:S(2)}) async-start(f16[4,192,512]{2,1,0:T(8,128)(2,1)} %get-tuple-element.5), calls=%async_computation.2 | async-start | bytes 1572864 | tf_op jit(solution)/shard_map/all_to_all | solution.py:59
  74.2 33.2 %all-to-all-done.2 = f16[4,192,512]{2,1,0:T(8,128)(2,1)S(1)} async-done(((f16[4,192,512]{2,1,0:T(8,128)(2,1)}), f16[4,192,512]{2,1,0:T(8,128)(2,1)S(1)}, u32[]{:S(2)}, u32[]{:S(2)}) %all-to-all-start.2) | async-done | bytes 786464 | tf_op jit(solution)/shard_map/all_to_all | solution.py:59
  107.4 1.0 bitcast_add_fusion
  (7 shorter events, 0.1 us)
Async XLA Ops:
  0.0 39.3 %copy-start = (s32[4,96]{1,0:T(4,128)S(1)}, s32[4,96]{1,0:T(4,128)}, u32[]{:S(2)}) copy-start(s32[4,96]{1,0:T(4,128)} %param.9) | copy-start | bytes 4612
  0.0 8.8 %collective-permute-start = (bf16[16,512]{1,0:T(8,128)(2,1)}, bf16[16,512]{1,0:T(8,128)(2,1)S(1)}, u32[]{:S(2)}, u32[]{:S(2)}) collective-permute-start(bf16[16,512]{1,0:T(8,128)(2,1)} %param.6), channel_id=1, source_target_pairs={{0,0},{97,1},{2,2},{99,3},{4,4},{101,5},{6,6},{103,7},{1,8},{96,9}... | collective-permute-start | bytes 49160 | tf_op jit(solution)/shard_map/ppermute | solution.py:42
  31.5 5.9 %copy-start.1 = (bf16[512,512]{1,0:T(8,128)(2,1)S(1)}, bf16[512,512]{1,0:T(8,128)(2,1)}, u32[]{:S(2)}) copy-start(bf16[512,512]{1,0:T(8,128)(2,1)} %param.5) | copy-start | bytes 1572868
  31.5 8.1 %copy-start.3 = (s32[4,4]{1,0:T(4,128)S(1)}, s32[4,4]{1,0:T(4,128)}, u32[]{:S(2)}) copy-start(s32[4,4]{1,0:T(4,128)} %param.8) | copy-start | bytes 196
  31.5 23.5 %all-to-all-start.1 = ((bf16[8,192,512]{2,1,0:T(8,128)(2,1)}), bf16[8,192,512]{2,1,0:T(8,128)(2,1)S(1)}, u32[]{:S(2)}, u32[]{:S(2)}) async-start(bf16[8,192,512]{2,1,0:T(8,128)(2,1)} %broadcast_in_dim.30), calls=%async_computation.1 | async-start | bytes 3145728 | tf_op jit(solution)/shard_map/all_to_all | solution.py:37
  37.4 18.4 %collective-permute-start.1 = (bf16[512,512]{1,0:T(8,128)(2,1)S(1)}, bf16[512,512]{1,0:T(8,128)(2,1)S(1)}, u32[]{:S(2)}, u32[]{:S(2)}) collective-permute-start(bf16[512,512]{1,0:T(8,128)(2,1)S(1)} %copy-done.1), channel_id=1, source_target_pairs={{0,1},{1,0},{2,3},{3,2},{4,5},{5,4},{6,7},{7,6},{8,9},{9,8},{10,11... | collective-permute-start | bytes 1572872 | tf_op jit(solution)/shard_map/ppermute | solution.py:32
  57.6 49.8 %copy-start.2 = (f32[512,192]{0,1:T(8,128)S(1)}, f32[512,192]{0,1:T(8,128)}, u32[]{:S(2)}) copy-start(f32[512,192]{0,1:T(8,128)} %param.7) | copy-start | bytes 1179652
  57.6 49.8 %all-to-all-start.2 = ((f16[4,192,512]{2,1,0:T(8,128)(2,1)}), f16[4,192,512]{2,1,0:T(8,128)(2,1)S(1)}, u32[]{:S(2)}, u32[]{:S(2)}) async-start(f16[4,192,512]{2,1,0:T(8,128)(2,1)} %get-tuple-element.5), calls=%async_computation.2 | async-start | bytes 1572864 | tf_op jit(solution)/shard_map/all_to_all | solution.py:59

commit v3 on v2

--- a/solution.py
+++ b/solution.py
@@ -15,7 +15,7 @@
 def deal():
     pairs = []
     for zl, x, yh, yl, q, j in np.ndindex(*SIZES):
-        source_row = 12 * (2 * x + j) + zl * 4 + yh
+        source_row = 12 * (2 * ((q + x) % 4) + j) + zl * 4 + yh
         source = source_row * 8 + q * 2 + (j ^ yl)
         target = int(np.ravel_multi_index((zl, x, yh, yl, q, j), SIZES))
         pairs.append((source, target))
@@ -44,6 +44,7 @@
     some = gather(piece, ("zl", "yh"), 12).reshape(192, 512)
     keep_int = lax.dynamic_slice(int_live, (q, 0), (1, 96)).reshape(4, 2, 12)
     keep_int = lax.dynamic_slice(keep_int, (0, j, 0), (4, 1, 12)).reshape(4, 12)
+    keep_int = lax.dynamic_slice(jnp.concatenate([keep_int] * 2), (q, 0), (4, 12))
     keep_int = jnp.repeat(keep_int, 16, axis=1).astype(jnp.float32)
     keep_amp = lax.dynamic_slice(amp_live, (0, q), (4, 1)).reshape(4)
     keep_amp = jnp.repeat(keep_amp, 128).astype(jnp.float32)
@@ -55,12 +56,12 @@
         total = contract(every[0], amplitudes) + contract(every[1], other)
         total = total.reshape(4, size, 512)
         total = total * (keep_int[:, rows, None] * keep_amp[None, None, :])
+        own = total[0]
         sent = (total * SCALE).astype(jnp.float16)
-        came = lax.all_to_all(sent, "zh", split_axis=0, concat_axis=0, tiled=True)
-        own = lax.dynamic_slice(total, (q, 0, 0), (1, size, 512))[0]
-        for kt in range(4):
-            term = came[kt].astype(jnp.float32) * (1.0 / SCALE)
-            own = own + jnp.where(kt == q, 0.0, term)
+        for by in (2, 1, 3):
+            pairs = [(i, (i + by) % 4) for i in range(4)]
+            came = lax.ppermute(sent[by], "zh", pairs)
+            own = own + came.astype(jnp.float32) * (1.0 / SCALE)
         outs.append(own)
     total = jnp.concatenate(outs, axis=0)
     return residual_in + jnp.transpose(total)

time: 109 us -> 100 us (0.917)
  waiting for transfers between devices: 49.9 us -> 35.3 us
  starting transfers between devices: 31.6 us -> 38.4 us
    all_to_all x1 -> x0, waiting for transfers between devices: 33.2 us -> none  [shards(): came = lax.all_to_all(sent, 'zh', split_axis=0, concat_axis=0, tiled=True)]
    ppermute x0 -> x3, starting transfers between devices: none -> 23.4 us  [shards(): came = lax.ppermute(sent[by], 'zh', pairs)]
    ppermute x0 -> x3, waiting for transfers between devices: none -> 18.6 us  [shards(): came = lax.ppermute(sent[by], 'zh', pairs)]
    all_to_all x1 -> x0, starting transfers between devices: 16.6 us -> none  [shards(): came = lax.all_to_all(sent, 'zh', split_axis=0, concat_axis=0, tiled=True)]
  transfers between devices with their start and end apart: 4 -> 6, of which waited for: 3 -> 3; matrix products, arithmetic and copies ran while one was open for 1% -> 1% of each run, Pallas kernels for 0% -> 0%
where the time goes in v3:
time: 100 us; the launch traced here: 99.7 us
  starting transfers between devices  38.4 us (38%)
  waiting for transfers between devices  35.3 us (35%)
  blocking collectives  21.3 us (21%)
  local copies, waits for them, and re-layouts  1.94 us (2%)
  other arithmetic  1.4 us (1%)
  matrix products  1.22 us (1%)
    ppermute x3, starting transfers between devices, shards(): came = lax.ppermute(sent[by], 'zh', pairs)  23.4 us
    all_to_all x1, blocking collectives, gather(): return lax.all_to_all(copies, axes, split_axis=0, concat_axis=0, tiled=True)  21.3 us
    ppermute x3, waiting for transfers between devices, shards(): came = lax.ppermute(sent[by], 'zh', pairs)  18.6 us
    all_to_all x1, waiting for transfers between devices, gather(): return lax.all_to_all(copies, axes, split_axis=0, concat_axis=0, tiled=True)  15.1 us
    ppermute x1, starting transfers between devices, shards(): piece = lax.ppermute(integrals, AXES, deal())  7.19 us
    all_to_all x1, starting transfers between devices, gather(): return lax.all_to_all(copies, axes, split_axis=0, concat_axis=0, tiled=True)  5.88 us
  transfers between devices with their start and end apart: 6, of which 3 were waited for; matrix products, arithmetic and copies ran while one was open for 1% of the time, Pallas kernels for 0%

profile of v3, /device:TPU:10, one launch (start us, length us, event | category | flops | bytes accessed | tf_op | source)
XLA Modules:
  0.0 99.7 jit_solution(10221445476841492350)
XLA Ops:
  0.0 7.2 %collective-permute-start = (bf16[16,512]{1,0:T(8,128)(2,1)}, bf16[16,512]{1,0:T(8,128)(2,1)S(1)}, u32[]{:S(2)}, u32[]{:S(2)}) collective-permute-start(bf16[16,512]{1,0:T(8,128)(2,1)} %param.6), channel_id=1, source_target_pairs={{0,0},{97,1},{194,2},{291,3},{388,4},{485,5},{582,6},{679,7},{1,8}... | collective-permute-start | bytes 49160 | tf_op jit(solution)/shard_map/ppermute | solution.py:42
  7.2 1.6 %collective-permute-done = bf16[16,512]{1,0:T(8,128)(2,1)S(1)} collective-permute-done((bf16[16,512]{1,0:T(8,128)(2,1)}, bf16[16,512]{1,0:T(8,128)(2,1)S(1)}, u32[]{:S(2)}, u32[]{:S(2)}) %collective-permute-start) | collective-permute-done | bytes 16416 | tf_op jit(solution)/shard_map/ppermute | solution.py:42
  8.9 21.3 %all_to_all.10 = bf16[12,16,512]{2,1,0:T(8,128)(2,1)S(1)} all-to-all(bf16[12,16,512]{2,1,0:T(8,128)(2,1)S(1)} %broadcast_in_dim.10), channel_id=1, replica_groups=mesh['zl'=3,'x'=4,'yh'=4,'yl'=2,'zh'=4,'core'=2] {'zl','yh'}, dimensions={0} | all-to-all | bytes 393216 | tf_op jit(solution)/shard_map/all_to_all | solution.py:37
  30.2 1.3 %broadcast_in_dim.23 = bf16[8,192,512]{2,1,0:T(8,128)(2,1)} broadcast(bf16[192,512]{1,0:T(8,128)(2,1)S(1)} %bitcast.36), dimensions={1,2} | broadcast | bytes 1769472 | tf_op jit(solution)/shard_map/broadcast_in_dim | solution.py:36
  31.5 5.9 %all-to-all-start.1 = ((bf16[8,192,512]{2,1,0:T(8,128)(2,1)}), bf16[8,192,512]{2,1,0:T(8,128)(2,1)S(1)}, u32[]{:S(2)}, u32[]{:S(2)}) async-start(bf16[8,192,512]{2,1,0:T(8,128)(2,1)} %broadcast_in_dim.23), calls=%async_computation.1 | async-start | bytes 3145728 | tf_op jit(solution)/shard_map/all_to_all | solution.py:37
  37.4 1.9 %collective-permute-start.1 = (bf16[512,512]{1,0:T(8,128)(2,1)S(1)}, bf16[512,512]{1,0:T(8,128)(2,1)S(1)}, u32[]{:S(2)}, u32[]{:S(2)}) collective-permute-start(bf16[512,512]{1,0:T(8,128)(2,1)S(1)} %copy-done.1), channel_id=1, source_target_pairs={{0,1},{1,0},{2,3},{3,2},{4,5},{5,4},{6,7},{7,6},{8,9},{9,8},{10,11... | collective-permute-start | bytes 1572872 | tf_op jit(solution)/shard_map/ppermute | solution.py:32
  39.3 0.2 convert_reduce_fusion
  39.5 0.1 reshape.33
  39.6 0.1 broadcast_in_dim.24
  39.7 0.1 convert_element_type.38
  39.8 0.1 broadcast_bitcast_fusion
  39.9 15.1 %all-to-all-done.1 = bf16[8,192,512]{2,1,0:T(8,128)(2,1)S(1)} async-done(((bf16[8,192,512]{2,1,0:T(8,128)(2,1)}), bf16[8,192,512]{2,1,0:T(8,128)(2,1)S(1)}, u32[]{:S(2)}, u32[]{:S(2)}) %all-to-all-start.1) | async-done | bytes 1572896 | tf_op jit(solution)/shard_map/all_to_all | solution.py:37
  54.9 0.2 fusion.6
  55.1 0.6 fusion.7
  55.7 0.0 collective-permute-done.1
  55.7 0.6 convolution_add_fusion
  56.4 0.0 copy-start.2
  56.4 0.3 multiply_convert_fusion
  56.7 0.1 slice_bitcast_fusion.3
  56.8 15.8 %collective-permute-start.2 = (f16[192,512]{1,0:T(8,128)(2,1)S(1)}, f16[192,512]{1,0:T(8,128)(2,1)S(1)}, u32[]{:S(2)}, u32[]{:S(2)}) collective-permute-start(f16[192,512]{1,0:T(8,128)(2,1)S(1)} %get-tuple-element.9), channel_id=1, source_target_pairs={{0,4},{2,6},{4,0},{6,2},{1,5},{3,7},{5,1},{7,3},{8,12},{10,14},{12... | collective-permute-start | bytes 589832 | tf_op jit(solution)/shard_map/ppermute | solution.py:63
  72.6 1.9 %collective-permute-start.4 = (f16[192,512]{1,0:T(8,128)(2,1)S(1)}, f16[192,512]{1,0:T(8,128)(2,1)S(1)}, u32[]{:S(2)}, u32[]{:S(2)}) collective-permute-start(f16[192,512]{1,0:T(8,128)(2,1)S(1)} %get-tuple-element.10), channel_id=1, source_target_pairs={{0,6},{2,0},{4,2},{6,4},{1,7},{3,1},{5,3},{7,5},{8,14},{10,8},{12,... | collective-permute-start | bytes 589832 | tf_op jit(solution)/shard_map/ppermute | solution.py:63
  74.5 5.7 %collective-permute-start.3 = (f16[192,512]{1,0:T(8,128)(2,1)S(1)}, f16[192,512]{1,0:T(8,128)(2,1)S(1)}, u32[]{:S(2)}, u32[]{:S(2)}) collective-permute-start(f16[192,512]{1,0:T(8,128)(2,1)S(1)} %get-tuple-element.11), channel_id=1, source_target_pairs={{0,2},{2,4},{4,6},{6,0},{1,3},{3,5},{5,7},{7,1},{8,10},{10,12},{12... | collective-permute-start | bytes 589832 | tf_op jit(solution)/shard_map/ppermute | solution.py:63
  80.2 18.6 %collective-permute-done.4 = f16[192,512]{1,0:T(8,128)(2,1)S(1)} collective-permute-done((f16[192,512]{1,0:T(8,128)(2,1)S(1)}, f16[192,512]{1,0:T(8,128)(2,1)S(1)}, u32[]{:S(2)}, u32[]{:S(2)}) %collective-permute-start.4) | collective-permute-done | bytes 196640 | tf_op jit(solution)/shard_map/ppermute | solution.py:63
  98.9 0.9 fusion.4
  (14 shorter events, 0.1 us)
Async XLA Ops:
  0.0 39.5 %copy-start = (s32[4,96]{1,0:T(4,128)S(1)}, s32[4,96]{1,0:T(4,128)}, u32[]{:S(2)}) copy-start(s32[4,96]{1,0:T(4,128)} %param.9) | copy-start | bytes 4612
  0.0 8.8 %collective-permute-start = (bf16[16,512]{1,0:T(8,128)(2,1)}, bf16[16,512]{1,0:T(8,128)(2,1)S(1)}, u32[]{:S(2)}, u32[]{:S(2)}) collective-permute-start(bf16[16,512]{1,0:T(8,128)(2,1)} %param.6), channel_id=1, source_target_pairs={{0,0},{97,1},{194,2},{291,3},{388,4},{485,5},{582,6},{679,7},{1,8}... | collective-permute-start | bytes 49160 | tf_op jit(solution)/shard_map/ppermute | solution.py:42
  31.5 5.9 %copy-start.1 = (bf16[512,512]{1,0:T(8,128)(2,1)S(1)}, bf16[512,512]{1,0:T(8,128)(2,1)}, u32[]{:S(2)}) copy-start(bf16[512,512]{1,0:T(8,128)(2,1)} %param.5) | copy-start | bytes 1572868
  31.5 7.8 %copy-start.3 = (s32[4,4]{1,0:T(4,128)S(1)}, s32[4,4]{1,0:T(4,128)}, u32[]{:S(2)}) copy-start(s32[4,4]{1,0:T(4,128)} %param.8) | copy-start | bytes 196
  31.5 23.5 %all-to-all-start.1 = ((bf16[8,192,512]{2,1,0:T(8,128)(2,1)}), bf16[8,192,512]{2,1,0:T(8,128)(2,1)S(1)}, u32[]{:S(2)}, u32[]{:S(2)}) async-start(bf16[8,192,512]{2,1,0:T(8,128)(2,1)} %broadcast_in_dim.23), calls=%async_computation.1 | async-start | bytes 3145728 | tf_op jit(solution)/shard_map/all_to_all | solution.py:37
  37.4 18.4 %collective-permute-start.1 = (bf16[512,512]{1,0:T(8,128)(2,1)S(1)}, bf16[512,512]{1,0:T(8,128)(2,1)S(1)}, u32[]{:S(2)}, u32[]{:S(2)}) collective-permute-start(bf16[512,512]{1,0:T(8,128)(2,1)S(1)} %copy-done.1), channel_id=1, source_target_pairs={{0,1},{1,0},{2,3},{3,2},{4,5},{5,4},{6,7},{7,6},{8,9},{9,8},{10,11... | collective-permute-start | bytes 1572872 | tf_op jit(solution)/shard_map/ppermute | solution.py:32
  56.4 42.5 %copy-start.2 = (f32[512,192]{0,1:T(8,128)S(1)}, f32[512,192]{0,1:T(8,128)}, u32[]{:S(2)}) copy-start(f32[512,192]{0,1:T(8,128)} %param.7) | copy-start | bytes 1179652
  56.8 23.4 %collective-permute-start.2 = (f16[192,512]{1,0:T(8,128)(2,1)S(1)}, f16[192,512]{1,0:T(8,128)(2,1)S(1)}, u32[]{:S(2)}, u32[]{:S(2)}) collective-permute-start(f16[192,512]{1,0:T(8,128)(2,1)S(1)} %get-tuple-element.9), channel_id=1, source_target_pairs={{0,4},{2,6},{4,0},{6,2},{1,5},{3,7},{5,1},{7,3},{8,12},{10,14},{12... | collective-permute-start | bytes 589832 | tf_op jit(solution)/shard_map/ppermute | solution.py:63
  72.6 26.3 %collective-permute-start.4 = (f16[192,512]{1,0:T(8,128)(2,1)S(1)}, f16[192,512]{1,0:T(8,128)(2,1)S(1)}, u32[]{:S(2)}, u32[]{:S(2)}) collective-permute-start(f16[192,512]{1,0:T(8,128)(2,1)S(1)} %get-tuple-element.10), channel_id=1, source_target_pairs={{0,6},{2,0},{4,2},{6,4},{1,7},{3,1},{5,3},{7,5},{8,14},{10,8},{12,... | collective-permute-start | bytes 589832 | tf_op jit(solution)/shard_map/ppermute | solution.py:63
  74.5 24.4 %collective-permute-start.3 = (f16[192,512]{1,0:T(8,128)(2,1)S(1)}, f16[192,512]{1,0:T(8,128)(2,1)S(1)}, u32[]{:S(2)}, u32[]{:S(2)}) collective-permute-start(f16[192,512]{1,0:T(8,128)(2,1)S(1)} %get-tuple-element.11), channel_id=1, source_target_pairs={{0,2},{2,4},{4,6},{6,0},{1,3},{3,5},{5,7},{7,1},{8,10},{10,12},{12... | collective-permute-start | bytes 589832 | tf_op jit(solution)/shard_map/ppermute | solution.py:63

commit v4 on v2

v4 whole, which is shorter than its diff:
```python
import jax
import jax.numpy as jnp
from jax import lax
from jax.sharding import Mesh, PartitionSpec as P

AXES = ("zl", "x", "yh", "yl", "zh", "core")
SIZES = (3, 4, 4, 2, 4, 2)
ROW = ("zl", "x", "yh", "yl")
COL = ("zh", "core")
SCALE = 32.0


def contract(left, right):
    return lax.dot_general(
        left, right, (((1,), (1,)), ((), ())), preferred_element_type=jnp.float32
    )


def shift(value, by):
    pairs = []
    for i in range(4):
        pairs.append((2 * i, 2 * ((i + by) % 4)))
        pairs.append((2 * i + 1, 2 * ((i - by) % 4) + 1))
    return lax.ppermute(value, COL, pairs)


def swap(value):
    return lax.ppermute(value, "core", [(0, 1), (1, 0)])


def gather(piece, axes, peers):
    copies = jnp.broadcast_to(piece[None], (peers,) + piece.shape)
    return lax.all_to_all(copies, axes, split_axis=0, concat_axis=0, tiled=True)


def shards(amplitudes, integrals, residual_in, amp_live, int_live):
    q, j = lax.axis_index("zh"), lax.axis_index("core")
    some = gather(integrals, ("zl", "yh"), 12).reshape(192, 512)
    other = swap(amplitudes)
    some, other = lax.optimization_barrier((some, other))
    every = gather(some, ("yl", "x"), 8).reshape(2, 4, 3, 4, 16, 512)
    every = every.transpose(2, 1, 3, 0, 4, 5).reshape(4, 2, 192, 512)
    theirs = swap(lax.dynamic_slice(every, (0, 1 - j, 0, 0), (4, 1, 192, 512)))
    mine = lax.dynamic_slice(every, (0, j, 0, 0), (4, 1, 192, 512))
    total = contract(mine.reshape(768, 512), amplitudes)
    total = total + contract(theirs.reshape(768, 512), other)
    total = total.reshape(4, 192, 512)
    keep_amp = lax.dynamic_slice(amp_live, (0, q), (4, 1)).reshape(4)
    keep_amp = jnp.repeat(keep_amp, 128).astype(jnp.float32)[None, :]

    def product(slot):
        n = (q + slot) % 4
        keep_int = lax.dynamic_slice(int_live, (q, 12 * (2 * n + j)), (1, 12)).reshape(12)
        keep_int = jnp.repeat(keep_int, 16).astype(jnp.float32)[:, None]
        return lax.dynamic_slice(total, (n, 0, 0), (1, 192, 512))[0] * (keep_int * keep_amp)

    ahead = 1 + 2 * j
    relayed = shift((product(2) * SCALE).astype(jnp.float16), 1)
    behind = shift((product(4 - ahead) * SCALE).astype(jnp.float16), -1)
    both = product(ahead) * SCALE + relayed.astype(jnp.float32)
    both = shift(both.astype(jnp.float16), 1)
    came = behind.astype(jnp.float32) + both.astype(jnp.float32)
    return residual_in + jnp.transpose(product(0) + came * (1.0 / SCALE))


def solution(mesh):
    fine = Mesh(mesh.devices.reshape(SIZES), AXES)
    in_specs = (P(ROW, COL), P(ROW, COL), P(ROW, COL), P(ROW, None), P())
    return jax.shard_map(
        shards, mesh=fine, in_specs=in_specs, out_specs=P(ROW, COL), check_vma=False
    )
```

time: 109 us -> 90.2 us (0.83)
  the two profiles are of different devices: /device:TPU:10 before, /device:TPU:56 now
where the time goes in v4:
time: 90.2 us; the launch traced here: 89.3 us
  starting transfers between devices  46.9 us (52%)
  waiting for transfers between devices  35.9 us (40%)
  local copies, waits for them, and re-layouts  3.64 us (4%)
  other arithmetic  1.49 us (2%)
  matrix products  1.21 us (1%)
    ppermute x3, starting transfers between devices, shift(): return lax.ppermute(value, COL, pairs)  25.7 us
    all_to_all x2, waiting for transfers between devices, gather(): return lax.all_to_all(copies, axes, split_axis=0, concat_axis=0, tiled=True)  21.1 us
    all_to_all x2, starting transfers between devices, gather(): return lax.all_to_all(copies, axes, split_axis=0, concat_axis=0, tiled=True)  17.2 us
    ppermute x3, waiting for transfers between devices, shift(): return lax.ppermute(value, COL, pairs)  11.8 us
    ppermute x2, starting transfers between devices, swap(): return lax.ppermute(value, 'core', [(0, 1), (1, 0)])  3.96 us
    ppermute x2, waiting for transfers between devices, swap(): return lax.ppermute(value, 'core', [(0, 1), (1, 0)])  2.98 us
    broadcast_in_dim x2, local copies, waits for them, and re-layouts, gather(): copies = jnp.broadcast_to(piece[None], (peers,) + piece.shape)  2.7 us
  transfers between devices with their start and end apart: 7, of which 6 were waited for; matrix products, arithmetic and copies ran while one was open for 2% of the time, Pallas kernels for 0%

profile of v4, /device:TPU:56, one launch (start us, length us, event | category | flops | bytes accessed | tf_op | source)
XLA Modules:
  0.0 89.3 jit_solution(484226145878894125)
XLA Ops:
  0.0 1.4 %broadcast_in_dim.14 = bf16[12,16,512]{2,1,0:T(8,128)(2,1)} broadcast(bf16[16,512]{1,0:T(8,128)(2,1)} %param.6), dimensions={1,2} | broadcast | bytes 212992 | tf_op jit(solution)/shard_map/broadcast_in_dim | solution.py:32
  1.4 10.6 %all-to-all-start = ((bf16[12,16,512]{2,1,0:T(8,128)(2,1)}), bf16[12,16,512]{2,1,0:T(8,128)(2,1)S(1)}, u32[]{:S(2)}, u32[]{:S(2)}) async-start(bf16[12,16,512]{2,1,0:T(8,128)(2,1)} %broadcast_in_dim.14), calls=%async_computation | async-start | bytes 393216 | tf_op jit(solution)/shard_map/all_to_all | solution.py:33
  12.0 1.9 %collective-permute-start = (bf16[512,512]{1,0:T(8,128)(2,1)}, bf16[512,512]{1,0:T(8,128)(2,1)S(1)}, u32[]{:S(2)}, u32[]{:S(2)}) collective-permute-start(bf16[512,512]{1,0:T(8,128)(2,1)} %param.5), channel_id=1, source_target_pairs={{0,1},{1,0},{2,3},{3,2},{4,5},{5,4},{6,7},{7,6},{8,9},{9,8},{10,11... | collective-permute-start | bytes 1572872 | tf_op jit(solution)/shard_map/ppermute | solution.py:28
  13.9 2.1 %collective-permute-done = bf16[512,512]{1,0:T(8,128)(2,1)S(1)} collective-permute-done((bf16[512,512]{1,0:T(8,128)(2,1)}, bf16[512,512]{1,0:T(8,128)(2,1)S(1)}, u32[]{:S(2)}, u32[]{:S(2)}) %collective-permute-start) | collective-permute-done | bytes 524320 | tf_op jit(solution)/shard_map/ppermute | solution.py:28
  16.0 3.4 %all-to-all-done = bf16[12,16,512]{2,1,0:T(8,128)(2,1)S(1)} async-done(((bf16[12,16,512]{2,1,0:T(8,128)(2,1)}), bf16[12,16,512]{2,1,0:T(8,128)(2,1)S(1)}, u32[]{:S(2)}, u32[]{:S(2)}) %all-to-all-start) | async-done | bytes 196640 | tf_op jit(solution)/shard_map/all_to_all | solution.py:33
  19.5 1.3 %broadcast_in_dim.15 = bf16[8,192,512]{2,1,0:T(8,128)(2,1)} broadcast(bf16[192,512]{1,0:T(8,128)(2,1)S(1)} %bitcast.56), dimensions={1,2} | broadcast | bytes 1769472 | tf_op jit(solution)/shard_map/broadcast_in_dim | solution.py:32
  20.8 6.6 %all-to-all-start.1 = ((bf16[8,192,512]{2,1,0:T(8,128)(2,1)}), bf16[8,192,512]{2,1,0:T(8,128)(2,1)S(1)}, u32[]{:S(2)}, u32[]{:S(2)}) async-start(bf16[8,192,512]{2,1,0:T(8,128)(2,1)} %broadcast_in_dim.15), calls=%async_computation.1 | async-start | bytes 3145728 | tf_op jit(solution)/shard_map/all_to_all | solution.py:33
  27.4 17.7 %all-to-all-done.1 = bf16[8,192,512]{2,1,0:T(8,128)(2,1)S(1)} async-done(((bf16[8,192,512]{2,1,0:T(8,128)(2,1)}), bf16[8,192,512]{2,1,0:T(8,128)(2,1)S(1)}, u32[]{:S(2)}, u32[]{:S(2)}) %all-to-all-start.1) | async-done | bytes 1572896 | tf_op jit(solution)/shard_map/all_to_all | solution.py:33
  45.0 0.1 copy.6
  45.2 0.1 constant_dynamic-slice_fusion
  45.3 2.1 %collective-permute-start.1 = (bf16[4,1,192,512]{3,2,1,0:T(8,128)(2,1)S(1)}, bf16[4,1,192,512]{3,2,1,0:T(8,128)(2,1)S(1)}, u32[]{:S(2)}, u32[]{:S(2)}) collective-permute-start(bf16[4,1,192,512]{3,2,1,0:T(8,128)(2,1)S(1)} %get-tuple-element.11), channel_id=1, source_target_pairs={{0,1},{1,0},{2,3},{3,2},{4,5},{5,4},{6,7},{7,6},{8,9},{9,8},{10,11... | collective-permute-start | bytes 2359304 | tf_op jit(solution)/shard_map/ppermute | solution.py:28
  47.5 0.1 convert_bitcast_fusion.3
  47.7 0.2 convert_reduce_fusion
  48.1 0.6 fusion.8
  48.7 0.9 collective-permute-done.1
  49.6 0.6 convolution_add_fusion
  50.2 0.2 fusion.6
  50.4 10.3 %collective-permute-start.3 = (f16[192,512]{1,0:T(8,128)(2,1)S(1)}, f16[192,512]{1,0:T(8,128)(2,1)S(1)}, u32[]{:S(2)}, u32[]{:S(2)}) collective-permute-start(f16[192,512]{1,0:T(8,128)(2,1)S(1)} %get-tuple-element.10), channel_id=1, source_target_pairs={{0,2},{1,7},{2,4},{3,1},{4,6},{5,3},{6,0},{7,5},{8,10},{9,15},{10,... | collective-permute-start | bytes 589832 | tf_op jit(solution)/shard_map/ppermute | solution.py:24
  60.9 4.4 %collective-permute-start.2 = (f16[192,512]{1,0:T(8,128)(2,1)S(1)}, f16[192,512]{1,0:T(8,128)(2,1)S(1)}, u32[]{:S(2)}, u32[]{:S(2)}) collective-permute-start(f16[192,512]{1,0:T(8,128)(2,1)S(1)} %get-tuple-element.9), channel_id=1, source_target_pairs={{0,6},{1,3},{2,0},{3,5},{4,2},{5,7},{6,4},{7,1},{8,14},{9,11},{10,... | collective-permute-start | bytes 589832 | tf_op jit(solution)/shard_map/ppermute | solution.py:24
  65.3 1.8 %collective-permute-done.3 = f16[192,512]{1,0:T(8,128)(2,1)S(1)} collective-permute-done((f16[192,512]{1,0:T(8,128)(2,1)S(1)}, f16[192,512]{1,0:T(8,128)(2,1)S(1)}, u32[]{:S(2)}, u32[]{:S(2)}) %collective-permute-start.3) | collective-permute-done | bytes 196640 | tf_op jit(solution)/shard_map/ppermute | solution.py:24
  67.0 0.1 fusion.4
  67.2 11.0 %collective-permute-start.4 = (f16[192,512]{1,0:T(8,128)(2,1)S(1)}, f16[192,512]{1,0:T(8,128)(2,1)S(1)}, u32[]{:S(2)}, u32[]{:S(2)}) collective-permute-start(f16[192,512]{1,0:T(8,128)(2,1)S(1)} %fusion.4), channel_id=1, source_target_pairs={{0,2},{1,7},{2,4},{3,1},{4,6},{5,3},{6,0},{7,5},{8,10},{9,15},{10,... | collective-permute-start | bytes 589832 | tf_op jit(solution)/shard_map/ppermute | solution.py:24
  78.4 10.0 %collective-permute-done.4 = f16[192,512]{1,0:T(8,128)(2,1)S(1)} collective-permute-done((f16[192,512]{1,0:T(8,128)(2,1)S(1)}, f16[192,512]{1,0:T(8,128)(2,1)S(1)}, u32[]{:S(2)}, u32[]{:S(2)}) %collective-permute-start.4) | collective-permute-done | bytes 196640 | tf_op jit(solution)/shard_map/ppermute | solution.py:24
  88.4 0.9 bitcast_add_fusion
  (18 shorter events, 0.7 us)
Async XLA Ops:
  1.4 18.1 %all-to-all-start = ((bf16[12,16,512]{2,1,0:T(8,128)(2,1)}), bf16[12,16,512]{2,1,0:T(8,128)(2,1)S(1)}, u32[]{:S(2)}, u32[]{:S(2)}) async-start(bf16[12,16,512]{2,1,0:T(8,128)(2,1)} %broadcast_in_dim.14), calls=%async_computation | async-start | bytes 393216 | tf_op jit(solution)/shard_map/all_to_all | solution.py:33
  12.0 4.0 %collective-permute-start = (bf16[512,512]{1,0:T(8,128)(2,1)}, bf16[512,512]{1,0:T(8,128)(2,1)S(1)}, u32[]{:S(2)}, u32[]{:S(2)}) collective-permute-start(bf16[512,512]{1,0:T(8,128)(2,1)} %param.5), channel_id=1, source_target_pairs={{0,1},{1,0},{2,3},{3,2},{4,5},{5,4},{6,7},{7,6},{8,9},{9,8},{10,11... | collective-permute-start | bytes 1572872 | tf_op jit(solution)/shard_map/ppermute | solution.py:28
  20.8 24.3 %all-to-all-start.1 = ((bf16[8,192,512]{2,1,0:T(8,128)(2,1)}), bf16[8,192,512]{2,1,0:T(8,128)(2,1)S(1)}, u32[]{:S(2)}, u32[]{:S(2)}) async-start(bf16[8,192,512]{2,1,0:T(8,128)(2,1)} %broadcast_in_dim.15), calls=%async_computation.1 | async-start | bytes 3145728 | tf_op jit(solution)/shard_map/all_to_all | solution.py:33
  45.2 2.3 %copy-start.3 = (s32[4,96]{1,0:T(4,128)S(1)}, s32[4,96]{1,0:T(4,128)}, u32[]{:S(2)}) copy-start(s32[4,96]{1,0:T(4,128)} %param.9) | copy-start | bytes 4612
  45.2 2.5 %copy-start.2 = (s32[4,4]{1,0:T(4,128)S(1)}, s32[4,4]{1,0:T(4,128)}, u32[]{:S(2)}) copy-start(s32[4,4]{1,0:T(4,128)} %param.8) | copy-start | bytes 196
  45.2 2.9 %copy-start = (bf16[512,512]{1,0:T(8,128)(2,1)S(1)}, bf16[512,512]{1,0:T(8,128)(2,1)}, u32[]{:S(2)}) copy-start(bf16[512,512]{1,0:T(8,128)(2,1)} %param.5) | copy-start | bytes 1572868
  45.3 4.3 %collective-permute-start.1 = (bf16[4,1,192,512]{3,2,1,0:T(8,128)(2,1)S(1)}, bf16[4,1,192,512]{3,2,1,0:T(8,128)(2,1)S(1)}, u32[]{:S(2)}, u32[]{:S(2)}) collective-permute-start(bf16[4,1,192,512]{3,2,1,0:T(8,128)(2,1)S(1)} %get-tuple-element.11), channel_id=1, source_target_pairs={{0,1},{1,0},{2,3},{3,2},{4,5},{5,4},{6,7},{7,6},{8,9},{9,8},{10,11... | collective-permute-start | bytes 2359304 | tf_op jit(solution)/shard_map/ppermute | solution.py:28
  50.2 38.2 %copy-start.1 = (f32[512,192]{0,1:T(8,128)S(1)}, f32[512,192]{0,1:T(8,128)}, u32[]{:S(2)}) copy-start(f32[512,192]{0,1:T(8,128)} %param.7) | copy-start | bytes 1179652
  50.4 16.6 %collective-permute-start.3 = (f16[192,512]{1,0:T(8,128)(2,1)S(1)}, f16[192,512]{1,0:T(8,128)(2,1)S(1)}, u32[]{:S(2)}, u32[]{:S(2)}) collective-permute-start(f16[192,512]{1,0:T(8,128)(2,1)S(1)} %get-tuple-element.10), channel_id=1, source_target_pairs={{0,2},{1,7},{2,4},{3,1},{4,6},{5,3},{6,0},{7,5},{8,10},{9,15},{10,... | collective-permute-start | bytes 589832 | tf_op jit(solution)/shard_map/ppermute | solution.py:24
  60.9 17.5 %collective-permute-start.2 = (f16[192,512]{1,0:T(8,128)(2,1)S(1)}, f16[192,512]{1,0:T(8,128)(2,1)S(1)}, u32[]{:S(2)}, u32[]{:S(2)}) collective-permute-start(f16[192,512]{1,0:T(8,128)(2,1)S(1)} %get-tuple-element.9), channel_id=1, source_target_pairs={{0,6},{1,3},{2,0},{3,5},{4,2},{5,7},{6,4},{7,1},{8,14},{9,11},{10,... | collective-permute-start | bytes 589832 | tf_op jit(solution)/shard_map/ppermute | solution.py:24
  67.2 21.2 %collective-permute-start.4 = (f16[192,512]{1,0:T(8,128)(2,1)S(1)}, f16[192,512]{1,0:T(8,128)(2,1)S(1)}, u32[]{:S(2)}, u32[]{:S(2)}) collective-permute-start(f16[192,512]{1,0:T(8,128)(2,1)S(1)} %fusion.4), channel_id=1, source_target_pairs={{0,2},{1,7},{2,4},{3,1},{4,6},{5,3},{6,0},{7,5},{8,10},{9,15},{10,... | collective-permute-start | bytes 589832 | tf_op jit(solution)/shard_map/ppermute | solution.py:24

commit v5 on v4

--- a/solution.py
+++ b/solution.py
@@ -37,30 +37,33 @@
     q, j = lax.axis_index("zh"), lax.axis_index("core")
     some = gather(integrals, ("zl", "yh"), 12).reshape(192, 512)
     other = swap(amplitudes)
-    some, other = lax.optimization_barrier((some, other))
     every = gather(some, ("yl", "x"), 8).reshape(2, 4, 3, 4, 16, 512)
+    ahead = 1 + 2 * j
+    order = [(q + slot) % 4 for slot in (2, 4 - ahead, ahead, 0)]
+    keep_amp = lax.dynamic_slice(amp_live, (0, q), (4, 1)).reshape(4)
+    keep_amp = jnp.repeat(keep_amp, 128).astype(jnp.float32)[None, :]
+    keep_int = []
+    for n in order:
+        keep = lax.dynamic_slice(int_live, (q, 12 * (2 * n + j)), (1, 12)).reshape(12)
+        keep_int.append(jnp.repeat(keep, 16).astype(jnp.float32)[:, None])
+    every, other, keep_int, keep_amp = lax.optimization_barrier((every, other, keep_int, keep_amp))
     every = every.transpose(2, 1, 3, 0, 4, 5).reshape(4, 2, 192, 512)
     theirs = swap(lax.dynamic_slice(every, (0, 1 - j, 0, 0), (4, 1, 192, 512)))
     mine = lax.dynamic_slice(every, (0, j, 0, 0), (4, 1, 192, 512))
     total = contract(mine.reshape(768, 512), amplitudes)
     total = total + contract(theirs.reshape(768, 512), other)
     total = total.reshape(4, 192, 512)
-    keep_amp = lax.dynamic_slice(amp_live, (0, q), (4, 1)).reshape(4)
-    keep_amp = jnp.repeat(keep_amp, 128).astype(jnp.float32)[None, :]
-
-    def product(slot):
-        n = (q + slot) % 4
-        keep_int = lax.dynamic_slice(int_live, (q, 12 * (2 * n + j)), (1, 12)).reshape(12)
-        keep_int = jnp.repeat(keep_int, 16).astype(jnp.float32)[:, None]
-        return lax.dynamic_slice(total, (n, 0, 0), (1, 192, 512))[0] * (keep_int * keep_amp)
-
-    ahead = 1 + 2 * j
-    relayed = shift((product(2) * SCALE).astype(jnp.float16), 1)
-    behind = shift((product(4 - ahead) * SCALE).astype(jnp.float16), -1)
-    both = product(ahead) * SCALE + relayed.astype(jnp.float32)
+    products = []
+    for n, keep in zip(order, keep_int):
+        part = lax.dynamic_slice(total, (n, 0, 0), (1, 192, 512))[0]
+        products.append(part * (keep * keep_amp))
+    far, back, on, own = products
+    relayed = shift((far * SCALE).astype(jnp.float16), 1)
+    behind = shift((back * SCALE).astype(jnp.float16), -1)
+    both = on * SCALE + relayed.astype(jnp.float32)
     both = shift(both.astype(jnp.float16), 1)
     came = behind.astype(jnp.float32) + both.astype(jnp.float32)
-    return residual_in + jnp.transpose(product(0) + came * (1.0 / SCALE))
+    return residual_in + jnp.transpose(own + came * (1.0 / SCALE))
 
 
 def solution(mesh):

time: 90.2 us -> 89 us (0.987)
  blocking collectives: 0 us -> 17.9 us
  starting transfers between devices: 46.9 us -> 36 us
  waiting for transfers between devices: 35.9 us -> 28.9 us
    all_to_all x0 -> x1, blocking collectives: none -> 17.9 us  [gather(): return lax.all_to_all(copies, axes, split_axis=0, concat_axis=0, tiled=True)]
    all_to_all x2 -> x1, starting transfers between devices: 17.2 us -> 5.93 us  [gather(): return lax.all_to_all(copies, axes, split_axis=0, concat_axis=0, tiled=True)]
    all_to_all x2 -> x1, waiting for transfers between devices: 21.1 us -> 14.7 us  [gather(): return lax.all_to_all(copies, axes, split_axis=0, concat_axis=0, tiled=True)]
  transfers between devices with their start and end apart: 7 -> 6, of which waited for: 6 -> 5; matrix products, arithmetic and copies ran while one was open for 2% -> 2% of each run, Pallas kernels for 0% -> 0%
where the time goes in v5:
time: 89 us; the launch traced here: 88.6 us
  starting transfers between devices  36 us (40%)
  waiting for transfers between devices  28.9 us (32%)
  blocking collectives  17.9 us (20%)
  local copies, waits for them, and re-layouts  2.94 us (3%)
  other arithmetic  1.49 us (2%)
  matrix products  1.2 us (1%)
    ppermute x3, starting transfers between devices, shift(): return lax.ppermute(value, COL, pairs)  26.2 us
    all_to_all x1, blocking collectives, gather(): return lax.all_to_all(copies, axes, split_axis=0, concat_axis=0, tiled=True)  17.9 us
    all_to_all x1, waiting for transfers between devices, gather(): return lax.all_to_all(copies, axes, split_axis=0, concat_axis=0, tiled=True)  14.7 us
    ppermute x3, waiting for transfers between devices, shift(): return lax.ppermute(value, COL, pairs)  11.7 us
    all_to_all x1, starting transfers between devices, gather(): return lax.all_to_all(copies, axes, split_axis=0, concat_axis=0, tiled=True)  5.93 us
    ppermute x2, starting transfers between devices, swap(): return lax.ppermute(value, 'core', [(0, 1), (1, 0)])  3.83 us
    ppermute x2, waiting for transfers between devices, swap(): return lax.ppermute(value, 'core', [(0, 1), (1, 0)])  2.52 us
    broadcast_in_dim x2, local copies, waits for them, and re-layouts, gather(): copies = jnp.broadcast_to(piece[None], (peers,) + piece.shape)  2.02 us
  transfers between devices with their start and end apart: 6, of which 5 were waited for; matrix products, arithmetic and copies ran while one was open for 2% of the time, Pallas kernels for 0%

profile of v5, /device:TPU:56, one launch (start us, length us, event | category | flops | bytes accessed | tf_op | source)
XLA Modules:
  0.0 88.6 jit_solution(7879595607463036177)
XLA Ops:
  0.0 0.7 broadcast_in_dim.16
  0.7 17.9 %all_to_all.10 = bf16[12,16,512]{2,1,0:T(8,128)(2,1)S(1)} all-to-all(bf16[12,16,512]{2,1,0:T(8,128)(2,1)S(1)} %broadcast_in_dim.16), channel_id=1, replica_groups=mesh['zl'=3,'x'=4,'yh'=4,'yl'=2,'zh'=4,'core'=2] {'zl','yh'}, dimensions={0} | all-to-all | bytes 393216 | tf_op jit(solution)/shard_map/all_to_all | solution.py:33
  18.6 1.3 %broadcast_in_dim.35 = bf16[8,192,512]{2,1,0:T(8,128)(2,1)} broadcast(bf16[192,512]{1,0:T(8,128)(2,1)S(1)} %bitcast.59), dimensions={1,2} | broadcast | bytes 1769472 | tf_op jit(solution)/shard_map/broadcast_in_dim | solution.py:32
  19.9 5.9 %all-to-all-start.1 = ((bf16[8,192,512]{2,1,0:T(8,128)(2,1)}), bf16[8,192,512]{2,1,0:T(8,128)(2,1)S(1)}, u32[]{:S(2)}, u32[]{:S(2)}) async-start(bf16[8,192,512]{2,1,0:T(8,128)(2,1)} %broadcast_in_dim.35), calls=%async_computation.1 | async-start | bytes 3145728 | tf_op jit(solution)/shard_map/all_to_all | solution.py:33
  25.8 1.9 %collective-permute-start = (bf16[512,512]{1,0:T(8,128)(2,1)S(1)}, bf16[512,512]{1,0:T(8,128)(2,1)S(1)}, u32[]{:S(2)}, u32[]{:S(2)}) collective-permute-start(bf16[512,512]{1,0:T(8,128)(2,1)S(1)} %copy-done), channel_id=1, source_target_pairs={{0,1},{1,0},{2,3},{3,2},{4,5},{5,4},{6,7},{7,6},{8,9},{9,8},{10,11... | collective-permute-start | bytes 1572872 | tf_op jit(solution)/shard_map/ppermute | solution.py:28
  27.8 0.1 convert_bitcast_fusion
  28.4 0.1 convert_element_type.114
  28.5 0.2 convert_reduce_fusion
  28.7 0.9 %collective-permute-done = bf16[512,512]{1,0:T(8,128)(2,1)S(1)} collective-permute-done((bf16[512,512]{1,0:T(8,128)(2,1)S(1)}, bf16[512,512]{1,0:T(8,128)(2,1)S(1)}, u32[]{:S(2)}, u32[]{:S(2)}) %collective-permute-start) | collective-permute-done | bytes 524320 | tf_op jit(solution)/shard_map/ppermute | solution.py:28
  29.6 14.7 %all-to-all-done.1 = bf16[8,192,512]{2,1,0:T(8,128)(2,1)S(1)} async-done(((bf16[8,192,512]{2,1,0:T(8,128)(2,1)}), bf16[8,192,512]{2,1,0:T(8,128)(2,1)S(1)}, u32[]{:S(2)}, u32[]{:S(2)}) %all-to-all-start.1) | async-done | bytes 1572896 | tf_op jit(solution)/shard_map/all_to_all | solution.py:33
  44.3 0.1 copy.6
  44.5 0.1 constant_dynamic-slice_fusion
  44.6 1.9 %collective-permute-start.1 = (bf16[4,1,192,512]{3,2,1,0:T(8,128)(2,1)S(1)}, bf16[4,1,192,512]{3,2,1,0:T(8,128)(2,1)S(1)}, u32[]{:S(2)}, u32[]{:S(2)}) collective-permute-start(bf16[4,1,192,512]{3,2,1,0:T(8,128)(2,1)S(1)} %get-tuple-element.21), channel_id=1, source_target_pairs={{0,1},{1,0},{2,3},{3,2},{4,5},{5,4},{6,7},{7,6},{8,9},{9,8},{10,11... | collective-permute-start | bytes 2359304 | tf_op jit(solution)/shard_map/ppermute | solution.py:28
  46.5 0.6 fusion.8
  47.1 1.6 %collective-permute-done.1 = bf16[4,1,192,512]{3,2,1,0:T(8,128)(2,1)S(1)} collective-permute-done((bf16[4,1,192,512]{3,2,1,0:T(8,128)(2,1)S(1)}, bf16[4,1,192,512]{3,2,1,0:T(8,128)(2,1)S(1)}, u32[]{:S(2)}, u32[]{:S(2)}) %collective-permute-start.1) | collective-permute-done | bytes 786464 | tf_op jit(solution)/shard_map/ppermute | solution.py:28
  48.8 0.6 convolution_add_fusion
  49.4 0.2 fusion.6
  49.6 10.3 %collective-permute-start.3 = (f16[192,512]{1,0:T(8,128)(2,1)S(1)}, f16[192,512]{1,0:T(8,128)(2,1)S(1)}, u32[]{:S(2)}, u32[]{:S(2)}) collective-permute-start(f16[192,512]{1,0:T(8,128)(2,1)S(1)} %get-tuple-element.20), channel_id=1, source_target_pairs={{0,2},{1,7},{2,4},{3,1},{4,6},{5,3},{6,0},{7,5},{8,10},{9,15},{10,... | collective-permute-start | bytes 589832 | tf_op jit(solution)/shard_map/ppermute | solution.py:24
  59.9 4.4 %collective-permute-start.2 = (f16[192,512]{1,0:T(8,128)(2,1)S(1)}, f16[192,512]{1,0:T(8,128)(2,1)S(1)}, u32[]{:S(2)}, u32[]{:S(2)}) collective-permute-start(f16[192,512]{1,0:T(8,128)(2,1)S(1)} %get-tuple-element.19), channel_id=1, source_target_pairs={{0,6},{1,3},{2,0},{3,5},{4,2},{5,7},{6,4},{7,1},{8,14},{9,11},{10,... | collective-permute-start | bytes 589832 | tf_op jit(solution)/shard_map/ppermute | solution.py:24
  64.3 1.9 %collective-permute-done.3 = f16[192,512]{1,0:T(8,128)(2,1)S(1)} collective-permute-done((f16[192,512]{1,0:T(8,128)(2,1)S(1)}, f16[192,512]{1,0:T(8,128)(2,1)S(1)}, u32[]{:S(2)}, u32[]{:S(2)}) %collective-permute-start.3) | collective-permute-done | bytes 196640 | tf_op jit(solution)/shard_map/ppermute | solution.py:24
  66.2 0.1 fusion.4
  66.3 11.6 %collective-permute-start.4 = (f16[192,512]{1,0:T(8,128)(2,1)S(1)}, f16[192,512]{1,0:T(8,128)(2,1)S(1)}, u32[]{:S(2)}, u32[]{:S(2)}) collective-permute-start(f16[192,512]{1,0:T(8,128)(2,1)S(1)} %fusion.4), channel_id=1, source_target_pairs={{0,2},{1,7},{2,4},{3,1},{4,6},{5,3},{6,0},{7,5},{8,10},{9,15},{10,... | collective-permute-start | bytes 589832 | tf_op jit(solution)/shard_map/ppermute | solution.py:24
  77.9 9.8 %collective-permute-done.4 = f16[192,512]{1,0:T(8,128)(2,1)S(1)} collective-permute-done((f16[192,512]{1,0:T(8,128)(2,1)S(1)}, f16[192,512]{1,0:T(8,128)(2,1)S(1)}, u32[]{:S(2)}, u32[]{:S(2)}) %collective-permute-start.4) | collective-permute-done | bytes 196640 | tf_op jit(solution)/shard_map/ppermute | solution.py:24
  87.7 0.9 bitcast_add_fusion
  (17 shorter events, 0.6 us)
Async XLA Ops:
  19.9 5.9 %copy-start = (bf16[512,512]{1,0:T(8,128)(2,1)S(1)}, bf16[512,512]{1,0:T(8,128)(2,1)}, u32[]{:S(2)}) copy-start(bf16[512,512]{1,0:T(8,128)(2,1)} %param.5) | copy-start | bytes 1572868
  19.9 7.9 %copy-start.3 = (s32[4,96]{1,0:T(4,128)S(1)}, s32[4,96]{1,0:T(4,128)}, u32[]{:S(2)}) copy-start(s32[4,96]{1,0:T(4,128)} %param.9) | copy-start | bytes 4612
  19.9 8.6 %copy-start.2 = (s32[4,4]{1,0:T(4,128)S(1)}, s32[4,4]{1,0:T(4,128)}, u32[]{:S(2)}) copy-start(s32[4,4]{1,0:T(4,128)} %param.8) | copy-start | bytes 196
  19.9 24.4 %all-to-all-start.1 = ((bf16[8,192,512]{2,1,0:T(8,128)(2,1)}), bf16[8,192,512]{2,1,0:T(8,128)(2,1)S(1)}, u32[]{:S(2)}, u32[]{:S(2)}) async-start(bf16[8,192,512]{2,1,0:T(8,128)(2,1)} %broadcast_in_dim.35), calls=%async_computation.1 | async-start | bytes 3145728 | tf_op jit(solution)/shard_map/all_to_all | solution.py:33
  25.8 3.8 %collective-permute-start = (bf16[512,512]{1,0:T(8,128)(2,1)S(1)}, bf16[512,512]{1,0:T(8,128)(2,1)S(1)}, u32[]{:S(2)}, u32[]{:S(2)}) collective-permute-start(bf16[512,512]{1,0:T(8,128)(2,1)S(1)} %copy-done), channel_id=1, source_target_pairs={{0,1},{1,0},{2,3},{3,2},{4,5},{5,4},{6,7},{7,6},{8,9},{9,8},{10,11... | collective-permute-start | bytes 1572872 | tf_op jit(solution)/shard_map/ppermute | solution.py:28
  44.6 4.2 %collective-permute-start.1 = (bf16[4,1,192,512]{3,2,1,0:T(8,128)(2,1)S(1)}, bf16[4,1,192,512]{3,2,1,0:T(8,128)(2,1)S(1)}, u32[]{:S(2)}, u32[]{:S(2)}) collective-permute-start(bf16[4,1,192,512]{3,2,1,0:T(8,128)(2,1)S(1)} %get-tuple-element.21), channel_id=1, source_target_pairs={{0,1},{1,0},{2,3},{3,2},{4,5},{5,4},{6,7},{7,6},{8,9},{9,8},{10,11... | collective-permute-start | bytes 2359304 | tf_op jit(solution)/shard_map/ppermute | solution.py:28
  49.4 38.3 %copy-start.1 = (f32[512,192]{0,1:T(8,128)S(1)}, f32[512,192]{0,1:T(8,128)}, u32[]{:S(2)}) copy-start(f32[512,192]{0,1:T(8,128)} %param.7) | copy-start | bytes 1179652
  49.6 16.6 %collective-permute-start.3 = (f16[192,512]{1,0:T(8,128)(2,1)S(1)}, f16[192,512]{1,0:T(8,128)(2,1)S(1)}, u32[]{:S(2)}, u32[]{:S(2)}) collective-permute-start(f16[192,512]{1,0:T(8,128)(2,1)S(1)} %get-tuple-element.20), channel_id=1, source_target_pairs={{0,2},{1,7},{2,4},{3,1},{4,6},{5,3},{6,0},{7,5},{8,10},{9,15},{10,... | collective-permute-start | bytes 589832 | tf_op jit(solution)/shard_map/ppermute | solution.py:24
  59.9 18.0 %collective-permute-start.2 = (f16[192,512]{1,0:T(8,128)(2,1)S(1)}, f16[192,512]{1,0:T(8,128)(2,1)S(1)}, u32[]{:S(2)}, u32[]{:S(2)}) collective-permute-start(f16[192,512]{1,0:T(8,128)(2,1)S(1)} %get-tuple-element.19), channel_id=1, source_target_pairs={{0,6},{1,3},{2,0},{3,5},{4,2},{5,7},{6,4},{7,1},{8,14},{9,11},{10,... | collective-permute-start | bytes 589832 | tf_op jit(solution)/shard_map/ppermute | solution.py:24
  66.3 21.4 %collective-permute-start.4 = (f16[192,512]{1,0:T(8,128)(2,1)S(1)}, f16[192,512]{1,0:T(8,128)(2,1)S(1)}, u32[]{:S(2)}, u32[]{:S(2)}) collective-permute-start(f16[192,512]{1,0:T(8,128)(2,1)S(1)} %fusion.4), channel_id=1, source_target_pairs={{0,2},{1,7},{2,4},{3,1},{4,6},{5,3},{6,0},{7,5},{8,10},{9,15},{10,... | collective-permute-start | bytes 589832 | tf_op jit(solution)/shard_map/ppermute | solution.py:24

commit v6 on v5

--- a/solution.py
+++ b/solution.py
@@ -7,7 +7,7 @@
 SIZES = (3, 4, 4, 2, 4, 2)
 ROW = ("zl", "x", "yh", "yl")
 COL = ("zh", "core")
-SCALE = 32.0
+LEAST = -100.0
 
 
 def contract(left, right):
@@ -26,6 +26,16 @@
 
 def swap(value):
     return lax.ppermute(value, "core", [(0, 1), (1, 0)])
+
+
+def pack(value, power):
+    scaled = (value * jnp.exp2(14.0 - power)).astype(jnp.float16)
+    return jnp.concatenate([scaled, jnp.broadcast_to(power, (16, 512)).astype(jnp.float16)])
+
+
+def unpack(message):
+    power = message[192:193].astype(jnp.float32)
+    return message[:192].astype(jnp.float32) * jnp.exp2(power - 14.0), power
 
 
 def gather(piece, axes, peers):
@@ -58,12 +68,13 @@
         part = lax.dynamic_slice(total, (n, 0, 0), (1, 192, 512))[0]
         products.append(part * (keep * keep_amp))
     far, back, on, own = products
-    relayed = shift((far * SCALE).astype(jnp.float16), 1)
-    behind = shift((back * SCALE).astype(jnp.float16), -1)
-    both = on * SCALE + relayed.astype(jnp.float32)
-    both = shift(both.astype(jnp.float16), 1)
-    came = behind.astype(jnp.float32) + both.astype(jnp.float32)
-    return residual_in + jnp.transpose(own + came * (1.0 / SCALE))
+    power = jnp.max(jnp.abs(total), axis=(0, 1))[None]
+    power = jnp.ceil(jnp.log2(jnp.maximum(power, 2.0**LEAST))) + 1.0
+    relayed = shift(pack(far, power), 1)
+    behind = shift(pack(back, power), -1)
+    value, other_power = unpack(relayed)
+    both = shift(pack(on + value, jnp.maximum(power, other_power) + 1.0), 1)
+    return residual_in + jnp.transpose(own + (unpack(behind)[0] + unpack(both)[0]))
 
 
 def solution(mesh):

time: 89 us -> 91.1 us (1.024)
  waiting for transfers between devices: 28.9 us -> 30.7 us
    ppermute x3, waiting for transfers between devices: 11.7 us -> 13.5 us  [shift(): return lax.ppermute(value, COL, pairs)]
where the time goes in v6:
time: 91.1 us; the launch traced here: 90.7 us
  starting transfers between devices  35.9 us (39%)
  waiting for transfers between devices  30.7 us (34%)
  blocking collectives  17.9 us (20%)
  local copies, waits for them, and re-layouts  2.95 us (3%)
  other arithmetic  1.72 us (2%)
  matrix products  1.22 us (1%)
    ppermute x3, starting transfers between devices, shift(): return lax.ppermute(value, COL, pairs)  26.1 us
    all_to_all x1, blocking collectives, gather(): return lax.all_to_all(copies, axes, split_axis=0, concat_axis=0, tiled=True)  17.9 us
    all_to_all x1, waiting for transfers between devices, gather(): return lax.all_to_all(copies, axes, split_axis=0, concat_axis=0, tiled=True)  14.7 us
    ppermute x3, waiting for transfers between devices, shift(): return lax.ppermute(value, COL, pairs)  13.5 us
    all_to_all x1, starting transfers between devices, gather(): return lax.all_to_all(copies, axes, split_axis=0, concat_axis=0, tiled=True)  5.93 us
    ppermute x2, starting transfers between devices, swap(): return lax.ppermute(value, 'core', [(0, 1), (1, 0)])  3.83 us
    ppermute x2, waiting for transfers between devices, swap(): return lax.ppermute(value, 'core', [(0, 1), (1, 0)])  2.52 us
    broadcast_in_dim x2, local copies, waits for them, and re-layouts, gather(): copies = jnp.broadcast_to(piece[None], (peers,) + piece.shape)  2.01 us
  transfers between devices with their start and end apart: 6, of which 5 were waited for; matrix products, arithmetic and copies ran while one was open for 2% of the time, Pallas kernels for 0%

profile of v6, /device:TPU:56, one launch (start us, length us, event | category | flops | bytes accessed | tf_op | source)
XLA Modules:
  0.0 90.7 jit_solution(8675428405039887547)
XLA Ops:
  0.0 0.7 broadcast_in_dim.20
  0.7 17.9 %all_to_all.10 = bf16[12,16,512]{2,1,0:T(8,128)(2,1)S(1)} all-to-all(bf16[12,16,512]{2,1,0:T(8,128)(2,1)S(1)} %broadcast_in_dim.20), channel_id=1, replica_groups=mesh['zl'=3,'x'=4,'yh'=4,'yl'=2,'zh'=4,'core'=2] {'zl','yh'}, dimensions={0} | all-to-all | bytes 393216 | tf_op jit(solution)/shard_map/all_to_all | solution.py:43
  18.6 1.3 %broadcast_in_dim.22 = bf16[8,192,512]{2,1,0:T(8,128)(2,1)} broadcast(bf16[192,512]{1,0:T(8,128)(2,1)S(1)} %bitcast.64), dimensions={1,2} | broadcast | bytes 1769472 | tf_op jit(solution)/shard_map/broadcast_in_dim | solution.py:42
  19.9 5.9 %all-to-all-start.1 = ((bf16[8,192,512]{2,1,0:T(8,128)(2,1)}), bf16[8,192,512]{2,1,0:T(8,128)(2,1)S(1)}, u32[]{:S(2)}, u32[]{:S(2)}) async-start(bf16[8,192,512]{2,1,0:T(8,128)(2,1)} %broadcast_in_dim.22), calls=%async_computation.1 | async-start | bytes 3145728 | tf_op jit(solution)/shard_map/all_to_all | solution.py:43
  25.8 1.9 %collective-permute-start = (bf16[512,512]{1,0:T(8,128)(2,1)S(1)}, bf16[512,512]{1,0:T(8,128)(2,1)S(1)}, u32[]{:S(2)}, u32[]{:S(2)}) collective-permute-start(bf16[512,512]{1,0:T(8,128)(2,1)S(1)} %copy-done), channel_id=1, source_target_pairs={{0,1},{1,0},{2,3},{3,2},{4,5},{5,4},{6,7},{7,6},{8,9},{9,8},{10,11... | collective-permute-start | bytes 1572872 | tf_op jit(solution)/shard_map/ppermute | solution.py:28
  27.8 0.1 convert_bitcast_fusion
  28.5 0.2 convert_reduce_fusion.1
  28.7 0.9 collective-permute-done
  29.6 14.7 %all-to-all-done.1 = bf16[8,192,512]{2,1,0:T(8,128)(2,1)S(1)} async-done(((bf16[8,192,512]{2,1,0:T(8,128)(2,1)}), bf16[8,192,512]{2,1,0:T(8,128)(2,1)S(1)}, u32[]{:S(2)}, u32[]{:S(2)}) %all-to-all-start.1) | async-done | bytes 1572896 | tf_op jit(solution)/shard_map/all_to_all | solution.py:43
  44.3 0.1 copy.6
  44.5 0.1 constant_dynamic-slice_fusion
  44.6 1.9 %collective-permute-start.1 = (bf16[4,1,192,512]{3,2,1,0:T(8,128)(2,1)S(1)}, bf16[4,1,192,512]{3,2,1,0:T(8,128)(2,1)S(1)}, u32[]{:S(2)}, u32[]{:S(2)}) collective-permute-start(bf16[4,1,192,512]{3,2,1,0:T(8,128)(2,1)S(1)} %get-tuple-element.23), channel_id=1, source_target_pairs={{0,1},{1,0},{2,3},{3,2},{4,5},{5,4},{6,7},{7,6},{8,9},{9,8},{10,11... | collective-permute-start | bytes 2359304 | tf_op jit(solution)/shard_map/ppermute | solution.py:28
  46.5 0.6 fusion.15
  47.1 1.6 %collective-permute-done.1 = bf16[4,1,192,512]{3,2,1,0:T(8,128)(2,1)S(1)} collective-permute-done((bf16[4,1,192,512]{3,2,1,0:T(8,128)(2,1)S(1)}, bf16[4,1,192,512]{3,2,1,0:T(8,128)(2,1)S(1)}, u32[]{:S(2)}, u32[]{:S(2)}) %collective-permute-start.1) | collective-permute-done | bytes 786464 | tf_op jit(solution)/shard_map/ppermute | solution.py:28
  48.8 0.6 abs_reduce_fusion
  49.4 0.2 fusion.6
  49.6 0.1 pad_maximum_fusion.1
  49.7 10.3 %collective-permute-start.3 = (f16[208,512]{1,0:T(8,128)(2,1)S(1)}, f16[208,512]{1,0:T(8,128)(2,1)S(1)}, u32[]{:S(2)}, u32[]{:S(2)}) collective-permute-start(f16[208,512]{1,0:T(8,128)(2,1)S(1)} %get-tuple-element.27), channel_id=1, source_target_pairs={{0,2},{1,7},{2,4},{3,1},{4,6},{5,3},{6,0},{7,5},{8,10},{9,15},{10,... | collective-permute-start | bytes 638984 | tf_op jit(solution)/shard_map/ppermute | solution.py:24
  60.1 4.4 %collective-permute-start.2 = (f16[208,512]{1,0:T(8,128)(2,1)S(1)}, f16[208,512]{1,0:T(8,128)(2,1)S(1)}, u32[]{:S(2)}, u32[]{:S(2)}) collective-permute-start(f16[208,512]{1,0:T(8,128)(2,1)S(1)} %get-tuple-element.26), channel_id=1, source_target_pairs={{0,6},{1,3},{2,0},{3,5},{4,2},{5,7},{6,4},{7,1},{8,14},{9,11},{10,... | collective-permute-start | bytes 638984 | tf_op jit(solution)/shard_map/ppermute | solution.py:24
  64.5 2.1 %collective-permute-done.3 = f16[208,512]{1,0:T(8,128)(2,1)S(1)} collective-permute-done((f16[208,512]{1,0:T(8,128)(2,1)S(1)}, f16[208,512]{1,0:T(8,128)(2,1)S(1)}, u32[]{:S(2)}, u32[]{:S(2)}) %collective-permute-start.3) | collective-permute-done | bytes 213024 | tf_op jit(solution)/shard_map/ppermute | solution.py:24
  66.5 0.1 fusion.4
  66.8 11.5 %collective-permute-start.4 = (f16[208,512]{1,0:T(8,128)(2,1)S(1)}, f16[208,512]{1,0:T(8,128)(2,1)S(1)}, u32[]{:S(2)}, u32[]{:S(2)}) collective-permute-start(f16[208,512]{1,0:T(8,128)(2,1)S(1)} %pad_maximum_fusion.2), channel_id=1, source_target_pairs={{0,2},{1,7},{2,4},{3,1},{4,6},{5,3},{6,0},{7,5},{8,10},{9,15},{10,... | collective-permute-start | bytes 638984 | tf_op jit(solution)/shard_map/ppermute | solution.py:24
  78.3 11.5 %collective-permute-done.4 = f16[208,512]{1,0:T(8,128)(2,1)S(1)} collective-permute-done((f16[208,512]{1,0:T(8,128)(2,1)S(1)}, f16[208,512]{1,0:T(8,128)(2,1)S(1)}, u32[]{:S(2)}, u32[]{:S(2)}) %collective-permute-start.4) | collective-permute-done | bytes 213024 | tf_op jit(solution)/shard_map/ppermute | solution.py:24
  89.8 0.9 bitcast_add_fusion
  (26 shorter events, 0.8 us)
Async XLA Ops:
  19.9 5.9 %copy-start = (bf16[512,512]{1,0:T(8,128)(2,1)S(1)}, bf16[512,512]{1,0:T(8,128)(2,1)}, u32[]{:S(2)}) copy-start(bf16[512,512]{1,0:T(8,128)(2,1)} %param.5) | copy-start | bytes 1572868
  19.9 7.9 %copy-start.3 = (s32[4,96]{1,0:T(4,128)S(1)}, s32[4,96]{1,0:T(4,128)}, u32[]{:S(2)}) copy-start(s32[4,96]{1,0:T(4,128)} %param.9) | copy-start | bytes 4612
  19.9 8.6 %copy-start.2 = (s32[4,4]{1,0:T(4,128)S(1)}, s32[4,4]{1,0:T(4,128)}, u32[]{:S(2)}) copy-start(s32[4,4]{1,0:T(4,128)} %param.8) | copy-start | bytes 196
  19.9 24.4 %all-to-all-start.1 = ((bf16[8,192,512]{2,1,0:T(8,128)(2,1)}), bf16[8,192,512]{2,1,0:T(8,128)(2,1)S(1)}, u32[]{:S(2)}, u32[]{:S(2)}) async-start(bf16[8,192,512]{2,1,0:T(8,128)(2,1)} %broadcast_in_dim.22), calls=%async_computation.1 | async-start | bytes 3145728 | tf_op jit(solution)/shard_map/all_to_all | solution.py:43
  25.8 3.8 %collective-permute-start = (bf16[512,512]{1,0:T(8,128)(2,1)S(1)}, bf16[512,512]{1,0:T(8,128)(2,1)S(1)}, u32[]{:S(2)}, u32[]{:S(2)}) collective-permute-start(bf16[512,512]{1,0:T(8,128)(2,1)S(1)} %copy-done), channel_id=1, source_target_pairs={{0,1},{1,0},{2,3},{3,2},{4,5},{5,4},{6,7},{7,6},{8,9},{9,8},{10,11... | collective-permute-start | bytes 1572872 | tf_op jit(solution)/shard_map/ppermute | solution.py:28
  44.6 4.2 %collective-permute-start.1 = (bf16[4,1,192,512]{3,2,1,0:T(8,128)(2,1)S(1)}, bf16[4,1,192,512]{3,2,1,0:T(8,128)(2,1)S(1)}, u32[]{:S(2)}, u32[]{:S(2)}) collective-permute-start(bf16[4,1,192,512]{3,2,1,0:T(8,128)(2,1)S(1)} %get-tuple-element.23), channel_id=1, source_target_pairs={{0,1},{1,0},{2,3},{3,2},{4,5},{5,4},{6,7},{7,6},{8,9},{9,8},{10,11... | collective-permute-start | bytes 2359304 | tf_op jit(solution)/shard_map/ppermute | solution.py:28
  49.4 40.4 %copy-start.1 = (f32[512,192]{0,1:T(8,128)S(1)}, f32[512,192]{0,1:T(8,128)}, u32[]{:S(2)}) copy-start(f32[512,192]{0,1:T(8,128)} %param.7) | copy-start | bytes 1179652
  49.7 16.8 %collective-permute-start.3 = (f16[208,512]{1,0:T(8,128)(2,1)S(1)}, f16[208,512]{1,0:T(8,128)(2,1)S(1)}, u32[]{:S(2)}, u32[]{:S(2)}) collective-permute-start(f16[208,512]{1,0:T(8,128)(2,1)S(1)} %get-tuple-element.27), channel_id=1, source_target_pairs={{0,2},{1,7},{2,4},{3,1},{4,6},{5,3},{6,0},{7,5},{8,10},{9,15},{10,... | collective-permute-start | bytes 638984 | tf_op jit(solution)/shard_map/ppermute | solution.py:24
  60.1 18.2 %collective-permute-start.2 = (f16[208,512]{1,0:T(8,128)(2,1)S(1)}, f16[208,512]{1,0:T(8,128)(2,1)S(1)}, u32[]{:S(2)}, u32[]{:S(2)}) collective-permute-start(f16[208,512]{1,0:T(8,128)(2,1)S(1)} %get-tuple-element.26), channel_id=1, source_target_pairs={{0,6},{1,3},{2,0},{3,5},{4,2},{5,7},{6,4},{7,1},{8,14},{9,11},{10,... | collective-permute-start | bytes 638984 | tf_op jit(solution)/shard_map/ppermute | solution.py:24
  66.8 23.0 %collective-permute-start.4 = (f16[208,512]{1,0:T(8,128)(2,1)S(1)}, f16[208,512]{1,0:T(8,128)(2,1)S(1)}, u32[]{:S(2)}, u32[]{:S(2)}) collective-permute-start(f16[208,512]{1,0:T(8,128)(2,1)S(1)} %pad_maximum_fusion.2), channel_id=1, source_target_pairs={{0,2},{1,7},{2,4},{3,1},{4,6},{5,3},{6,0},{7,5},{8,10},{9,15},{10,... | collective-permute-start | bytes 638984 | tf_op jit(solution)/shard_map/ppermute | solution.py:24
